TPU v7x, 256 devices: a whole 4x4x8 slice. The times are simulated.
256 devices in a mesh: blk: 16 (over x, y_hi, core), narrow: 16 (over y_lo, z).
Axes of the slice: x: 4, y: 4 (y_hi: 2, y_lo: 2; y = y_hi * 2 + y_lo), z: 8, core: 2. Of those that a mesh axis runs over, the one named last changes fastest.
Arguments:
- image_emb: bfloat16 [16384, 768], P(('blk', 'narrow')), as said below
- text_emb: bfloat16 [16384, 768], P(('blk', 'narrow')), as said below
- log_temp: float32 [1], replicated, may hold values from 1 to 2
- bias: float32 [1], replicated, may hold values from -4 to -2
Outputs:
- mean_loss: float32 [1], replicated
- grad_image: float32 [16384, 768], P(('blk', 'narrow'))
- grad_text: float32 [16384, 768], P(('blk', 'narrow'))
- scalar_grads: float32 [2], replicated
Inputs may be any that keep to these rules, and one draw needn't show every extreme that they name: `image_emb`: finite values. `text_emb`: finite values.
All inputs are finite; a program needn't handle non-finite values.
Results may differ from a plain program's by a relative error of at most 0.0053.
Values may be sent and summed in bfloat16 or wider, within the bound.
A program may use at most 64 MiB of HBM per device.

v0:
```python
import jax
import jax.numpy as jnp
from jax import lax
from jax.sharding import PartitionSpec as P


def unit_rows(values):
    widened = values.astype(jnp.float32)
    return widened * lax.rsqrt(jnp.sum(widened * widened, axis=-1, keepdims=True) + 1e-06)


def back_rows(values, upstream):
    widened = values.astype(jnp.float32)
    inverse = lax.rsqrt(jnp.sum(widened * widened, axis=-1, keepdims=True) + 1e-06)
    unit = widened * inverse
    return inverse * (upstream - unit * jnp.sum(unit * upstream, axis=-1, keepdims=True))


def pair_terms(first_rows, second_rows, first_index, second_index, temper, offset):
    products = lax.dot_general(
        first_rows, second_rows, (((1,), (1,)), ((), ())), preferred_element_type=jnp.float32
    )
    logits = temper * products + offset
    matched = (first_index[:, None] == second_index[None, :]).astype(jnp.float32)
    signed = 2.0 * matched - 1.0
    loss_sum = jnp.sum(jax.nn.softplus(-signed * logits))
    slopes = jax.nn.sigmoid(logits) - matched
    found = jnp.stack([loss_sum, jnp.sum(slopes), jnp.sum(slopes * (logits - offset))])
    return (found, slopes.astype(jnp.bfloat16))


def tile_plan(image_unit, text_unit, temper, offset, row_count):
    group_count = lax.axis_size("narrow")
    here_blk = lax.axis_index("blk")
    here_group = lax.axis_index("narrow")
    images_all = lax.all_gather(image_unit, "narrow", axis=0, tiled=True)
    texts_all = lax.all_gather(text_unit, "blk", axis=0, tiled=True)
    image_total = images_all.shape[0]
    text_total = texts_all.shape[0]
    width = image_unit.shape[1]
    image_first = here_blk * group_count * row_count
    positions = lax.iota(jnp.int32, text_total)
    text_index = (
        positions // row_count * group_count + here_group
    ) * row_count + positions % row_count
    step_rows = 512

    def tile_step(count, current):
        found, image_part, text_part = current
        start = count * step_rows
        rows = lax.dynamic_slice_in_dim(images_all, start, step_rows, 0)
        row_index = image_first + start + lax.iota(jnp.int32, step_rows)
        more, slopes_b = pair_terms(rows, texts_all, row_index, text_index, temper, offset)
        image_piece = temper * jnp.dot(slopes_b, texts_all, preferred_element_type=jnp.float32)
        image_part = lax.dynamic_update_slice_in_dim(image_part, image_piece, start, 0)
        text_part = text_part + temper * lax.dot_general(
            slopes_b, rows, (((0,), (0,)), ((), ())), preferred_element_type=jnp.float32
        )
        return (found + more, image_part, text_part)

    start_state = (
        jnp.zeros((3,), jnp.float32),
        jnp.zeros((image_total, width), jnp.float32),
        jnp.zeros((text_total, width), jnp.float32),
    )
    found, image_part, text_part = lax.fori_loop(
        0, image_total // step_rows, tile_step, start_state
    )
    image_grad = lax.psum_scatter(image_part, "narrow", scatter_dimension=0, tiled=True)
    text_grad_unit = lax.psum_scatter(text_part, "blk", scatter_dimension=0, tiled=True)
    return (found, image_grad, text_grad_unit)


def local(image_emb, text_emb, log_temp, bias):
    row_count = image_emb.shape[0]
    blk_count = lax.axis_size("blk")
    group_count = lax.axis_size("narrow")
    image_unit = unit_rows(image_emb).astype(jnp.bfloat16)
    text_unit = unit_rows(text_emb).astype(jnp.bfloat16)
    temper = jnp.exp(log_temp[0])
    offset = bias[0]
    found, image_grad, text_grad_unit = tile_plan(image_unit, text_unit, temper, offset, row_count)
    summed = lax.psum(found, ("blk", "narrow"))
    pairs = float(row_count * blk_count * group_count) ** 2
    mean_loss = jnp.reshape(summed[0] / pairs, (1,))
    scalar_grads = jnp.stack([summed[2], summed[1]]) / pairs
    grad_image = back_rows(image_emb, image_grad)
    grad_text = back_rows(text_emb, text_grad_unit)
    return (mean_loss, grad_image, grad_text, scalar_grads)


def solution(mesh):
    placed = (P(("blk", "narrow"), None), P(("blk", "narrow"), None), P(), P())
    return jax.shard_map(
        local,
        mesh=mesh,
        in_specs=placed,
        out_specs=(P(), P(("blk", "narrow"), None), P(("blk", "narrow"), None), P()),
        check_vma=False,
    )
```

profile of v0, /device:TPU:4, one launch (start us, length us, event | category | flops | bytes accessed | tf_op | source)
XLA Modules:
  0.0 332.5 jit_solution(3830420842984052896)
XLA Ops:
  7.2 0.0 all-gather.5.cloned.1.call-start
  7.2 1.0 fusion.41
  8.2 1.6 fusion.30
  9.9 0.0 all-gather.5.cloned.1.call-update
  9.9 0.0 all-gather.3.cloned.1.call-start
  9.9 1.0 fusion.37
  11.0 1.6 fusion.33
  12.6 0.0 all-gather.3.cloned.1.call-update
  12.6 0.0 reduce-scatter.5.cloned.1.call-start
  13.4 51.1 %all-gather.5.cloned.1.call-done = bf16[1024,768]{1,0:T(8,128)(2,1)} async-done(((bf16[64,768]{1,0:T(8,128)(2,1)}), bf16[1024,768]{1,0:T(8,128)(2,1)}) %all-gather.5.cloned.1.call-update) | async-done | bytes 1572880 | tf_op jit(solution)/shard_map/all_gather | solution.py:37
  64.5 73.1 %all-gather.3.cloned.1.call-done = bf16[1024,768]{1,0:T(8,128)(2,1)} async-done(((bf16[64,768]{1,0:T(8,128)(2,1)}), bf16[1024,768]{1,0:T(8,128)(2,1)}) %all-gather.3.cloned.1.call-update) | async-done | bytes 1572880 | tf_op jit(solution)/shard_map/all_gather | solution.py:36
  137.6 0.2 broadcast.84
  137.8 24.8 %while.20 = (s32[]{:T(128)}, f32[3]{0:T(128)S(1)}, f32[1024,768]{1,0:T(8,128)S(1)}, f32[1024,768]{1,0:T(8,128)}, s32[]{:T(128)}, /*index=5*/f32[]{:T(128)}, bf16...) while((s32[]{:T(128)}, f32[3]{0:T(128)S(1)}, ...), condition=%wide.region_6.7_spmd.clone, body=%wide.region_2.6_spmd.clone.sunk | while | flops 2438087168 | bytes 56649100 | solution.py:66
  137.8 0.0 copy-start.1
  137.9 0.0 copy-start.6
  137.9 6.5 %fusion.59 = (f32[]{:T(128)}, f32[]{:T(128)}, f32[]{:T(128)}, f32[512,1024]{1,0:T(8,128)S(1)}) fusion(s32[1024]{0:T(1024)S(1)} %fusion.58, s32[512]{0:T(512)S(1)} %iota_add_fusion.2, f32[]{:T(128)} %get-tuple-element.419, bf16[1024,768]{1,0:T(8,128)(2,1)} %get-tuple-element.418, bf16[1024,768]{1,0:T(8,128)(2,1)} %get-tuple-element.417, ...), kind=kOutput, calls=%fused_computation.9.clone.1 | convolution fusion | flops 817364992 | bytes 4463632 | tf_op jit(solution)/shard_map/while/body/eval_jaxpr/dot_general | solution.py:20
  144.4 2.0 fusion.60
  146.4 0.0 copy-done.1
  146.4 0.0 copy-done.6
  146.4 2.1 select_add_fusion.2
  148.5 0.0 copy-done.5
  148.5 0.0 copy-start.2
  148.5 1.3 multiply_dynamic-update-slice_fusion.2
  149.9 0.3 copy-done.2
  150.2 0.0 copy-start.6
  150.2 6.5 %fusion.59 = (f32[]{:T(128)}, f32[]{:T(128)}, f32[]{:T(128)}, f32[512,1024]{1,0:T(8,128)S(1)}) fusion(s32[1024]{0:T(1024)S(1)} %fusion.58, s32[512]{0:T(512)S(1)} %iota_add_fusion.2, f32[]{:T(128)} %get-tuple-element.419, bf16[1024,768]{1,0:T(8,128)(2,1)} %get-tuple-element.418, bf16[1024,768]{1,0:T(8,128)(2,1)} %get-tuple-element.417, ...), kind=kOutput, calls=%fused_computation.9.clone.1 | convolution fusion | flops 817364992 | bytes 4463632 | tf_op jit(solution)/shard_map/while/body/eval_jaxpr/dot_general | solution.py:20
  156.8 2.0 fusion.60
  158.8 0.0 copy-done.1
  158.8 0.0 copy-done.6
  158.8 2.1 select_add_fusion.2
  160.9 1.3 multiply_dynamic-update-slice_fusion.2
  162.2 0.3 copy-done.2
  162.6 0.0 reduce-scatter.5.cloned.1.call-update
  162.6 0.0 copy-start.3
  162.6 0.0 copy-start.4
  162.6 0.0 reduce-scatter.3.cloned.1.call-start
  162.7 1.6 copy-done
  164.3 0.0 reduce-scatter.3.cloned.1.call-update
  164.3 73.2 %psum.7 = f32[3]{0:T(128)S(1)} all-reduce(f32[3]{0:T(128)S(1)} %get-tuple-element.248), channel_id=1, replica_groups=mesh['blk'=16,'narrow'=16] {'blk','narrow'}, use_global_device_ids=true, to_apply=%region_7.8 | all-reduce | flops 3 | bytes 24 | tf_op jit(solution)/shard_map/psum | solution.py:83
  237.5 0.6 fusion.42
  238.8 1.9 maximum_multiply_fusion
  240.6 1.0 reduce-scatter.5.cloned.1.call-done
  241.6 1.1 fusion.38
  242.7 1.7 fusion.40
  244.4 77.6 %reduce-scatter.3.cloned.1.call-done = f32[64,768]{1,0:T(8,128)} async-done(((f32[1024,768]{1,0:T(8,128)}), f32[64,768]{1,0:T(8,128)}) %reduce-scatter.3.cloned.1.call-update) | async-done | bytes 196624 | tf_op jit(solution)/shard_map/reduce_scatter | solution.py:69
  322.0 0.0 copy-done.4
  322.0 1.1 fusion.34
  323.1 1.7 fusion.36
  (15 shorter events, 0.1 us)
Async XLA Ops:
  7.2 57.3 %all-gather.5.cloned.1.call-start = ((), (), s32[]{:S(2)}) async-start(), calls=%async_computation.3 | async-start | bytes 1671168 | tf_op jit(solution)/shard_map/all_gather | solution.py:37
  9.9 127.7 %all-gather.3.cloned.1.call-start = ((), (), s32[]{:S(2)}) async-start(), calls=%async_computation.2 | async-start | bytes 1671168 | tf_op jit(solution)/shard_map/all_gather | solution.py:36
  12.6 229.0 %reduce-scatter.5.cloned.1.call-start = ((), (), s32[]{:S(2)}) async-start(), calls=%async_computation.5 | async-start | bytes 3342336 | tf_op jit(solution)/shard_map/reduce_scatter | solution.py:70
  137.8 8.5 %copy-start.1 = (f32[1024,768]{1,0:T(8,128)S(1)}, f32[1024,768]{1,0:T(8,128)}, u32[]{:S(2)}) copy-start(f32[1024,768]{1,0:T(8,128)} %get-tuple-element.400) | copy-start | bytes 9437188 | tf_op jit(solution)/shard_map/while
  137.9 8.5 %copy-start.6 = (bf16[1024,768]{1,0:T(8,128)(2,1)S(1)}, bf16[1024,768]{1,0:T(8,128)(2,1)}, u32[]{:S(2)}) copy-start(bf16[1024,768]{1,0:T(8,128)(2,1)} %get-tuple-element.417) | copy-start | bytes 4718596 | tf_op jit(solution)/shard_map/while
  146.4 2.1 copy-start.5
  148.5 1.7 copy-start.2
  150.2 8.5 %copy-start.1 = (f32[1024,768]{1,0:T(8,128)S(1)}, f32[1024,768]{1,0:T(8,128)}, u32[]{:S(2)}) copy-start(f32[1024,768]{1,0:T(8,128)} %get-tuple-element.400) | copy-start | bytes 9437188 | tf_op jit(solution)/shard_map/while
  150.2 8.5 %copy-start.6 = (bf16[1024,768]{1,0:T(8,128)(2,1)S(1)}, bf16[1024,768]{1,0:T(8,128)(2,1)}, u32[]{:S(2)}) copy-start(bf16[1024,768]{1,0:T(8,128)(2,1)} %get-tuple-element.417) | copy-start | bytes 4718596 | tf_op jit(solution)/shard_map/while
  158.8 2.1 copy-start.5
  160.9 1.7 copy-start.2
  162.6 1.7 copy-start
  162.6 79.0 %copy-start.3 = (bf16[64,768]{1,0:T(8,128)(2,1)S(1)}, bf16[64,768]{1,0:T(8,128)(2,1)}, u32[]{:S(2)}) copy-start(bf16[64,768]{1,0:T(8,128)(2,1)} %param.7) | copy-start | bytes 294916
  162.6 159.4 %copy-start.4 = (bf16[64,768]{1,0:T(8,128)(2,1)S(1)}, bf16[64,768]{1,0:T(8,128)(2,1)}, u32[]{:S(2)}) copy-start(bf16[64,768]{1,0:T(8,128)(2,1)} %param.6) | copy-start | bytes 294916
  162.6 159.3 %reduce-scatter.3.cloned.1.call-start = ((), (), s32[]{:S(2)}) async-start(), calls=%async_computation.4 | async-start | bytes 3342336 | tf_op jit(solution)/shard_map/reduce_scatter | solution.py:69
Sparse Core Ops, SparseCore 0:
  11.3 53.1 all-gather.4
  66.9 70.6 all-gather.2
  162.7 78.8 reduce-scatter.4
  244.0 77.9 reduce-scatter.2
where the time goes:
time: 333 us; the launch traced here: 332 us
  waiting for transfers between devices  203 us (61%)
  blocking collectives  73.2 us (22%)
  matrix products  19.9 us (6%)
  other arithmetic  16.9 us (5%)
  between operations  16.3 us (5%)
    reduce_scatter x1, waiting for transfers between devices, tile_plan(): lax.psum_scatter(image_part, 'narrow', scatter_dimension=0, tiled=True)  77.6 us
    psum x1, blocking collectives, local(): summed = lax.psum(found, ('blk', 'narrow'))  73.2 us
    all_gather x1, waiting for transfers between devices, tile_plan(): images_all = lax.all_gather(image_unit, 'narrow', axis=0, tiled=True)  73.1 us
    all_gather x1, waiting for transfers between devices, tile_plan(): texts_all = lax.all_gather(text_unit, 'blk', axis=0, tiled=True)  51.1 us
    dot_general x2, matrix products, pair_terms(): lax.dot_general(first_rows, second_rows, (((1,), (1,)), ((), ())), prefer...  13 us
  transfers between devices with their start and end apart: 4, of which 4 were waited for; matrix products, arithmetic and copies ran while one was open for 2% of the time, Pallas kernels for 0%

commit v1 on v0

v1 whole, which is shorter than its diff:
```python
import math

import jax
import jax.numpy as jnp
from jax import lax
from jax.experimental import pallas as pl
from jax.experimental.pallas import tpu as pltpu
from jax.sharding import PartitionSpec as P

MESH = pl.DeviceIdType.MESH
ROWS, WIDTH = 64, 768
GROUP = 4 * ROWS
TOTAL = 16384
LOG2E = math.log2(math.e)


def ring(step, size):
    return min(step % size, -step % size)


PLANE = sorted(
    ((dx, dy) for dx in range(4) for dy in range(4)),
    key=lambda p: (ring(p[0], 4) + ring(p[1], 4), p),
)
COLUMN = sorted(range(8), key=lambda d: (ring(d, 8), d))
PLANE_BACK = [PLANE.index((-dx % 4, -dy % 4)) for dx, dy in PLANE]
COLUMN_BACK = [COLUMN.index(-d % 8) for d in COLUMN]


def text_rows(other, place):
    return (place // 2 * 4 + other * 2 + place % 2) * ROWS


def row_scale(values):
    return lax.rsqrt(jnp.sum(values * values, axis=-1, keepdims=True) + 1e-06)


def back_rows(values, upstream):
    inverse = row_scale(values)
    unit = values * inverse
    return inverse * (upstream - unit * jnp.sum(unit * upstream, axis=-1, keepdims=True))


def fold(values):
    return jnp.sum(jnp.reshape(values, (values.shape[0] // 8, 8, values.shape[1])), axis=0)


def kernel(
    image_ref, text_ref, temp_ref, bias_ref,
    grad_image_ref, grad_text_ref, scalars_ref,
    images, texts, slopes, slopes_t, sums,
    image_part, text_part, pair_part, image_own, text_own,
    image_in, text_in, pair_in, found_in, found_out,
    image_ss, image_rs, text_ss, text_rs, pair_ss, pair_rs,
    gi_ss, gi_rs, gt_ss, gt_rs, gp_ss, gp_rs, f_ss, f_rs,
):
    blk, narrow = lax.axis_index("blk"), lax.axis_index("narrow")
    x, core = lax.div(blk, 4), lax.rem(blk, 2)
    y = lax.rem(lax.div(blk, 2), 2) * 2 + lax.div(narrow, 8)
    z = lax.rem(narrow, 8)

    def device(dx, dy, dz, other):
        px, py, pz = lax.rem(x + dx, 4), lax.rem(y + dy, 4), lax.rem(z + dz, 8)
        pc = lax.rem(core + other, 2)
        return (px * 4 + lax.div(py, 2) * 2 + pc, lax.rem(py, 2) * 8 + pz)

    plane = [device(dx, dy, 0, 0) for dx, dy in PLANE]
    column = [device(0, 0, dz, 0) for dz in COLUMN]
    twin = device(0, 0, 0, 1)

    barrier = pltpu.get_barrier_semaphore()
    for peer in plane[1:] + column[1:] + [twin]:
        pl.semaphore_signal(barrier, inc=1, device_id=peer, device_id_type=MESH)

    image = image_ref[...].astype(jnp.float32)
    images[0:ROWS, :] = (image * row_scale(image)).astype(jnp.bfloat16)
    text = text_ref[...].astype(jnp.float32)
    texts[0:ROWS, :] = (text * row_scale(text)).astype(jnp.bfloat16)
    sums[...] = jnp.zeros_like(sums)
    temper = jnp.exp(jnp.full((1, 256), temp_ref[0], jnp.float32))
    offset = jnp.full((1, 256), bias_ref[0], jnp.float32)
    temper2, offset2 = temper * LOG2E, offset * LOG2E

    pl.semaphore_wait(barrier, len(plane) + len(column) - 1)

    started = []

    def send(src, dst, send_sem, recv_sem, peer):
        copy = pltpu.make_async_remote_copy(
            src_ref=src, dst_ref=dst, send_sem=send_sem, recv_sem=recv_sem,
            device_id=peer, device_id_type=MESH,
        )
        copy.start()
        started.append(copy)
        return copy

    def image_rows(place):
        return pl.ds(place * ROWS, ROWS)

    image_copies, text_copies, pair_copies = {}, {}, {}

    def send_text(place):
        back = COLUMN_BACK[place]
        text_copies[back] = send(
            texts.at[0:ROWS], texts.at[pl.ds(text_rows(0, back), ROWS)],
            text_ss.at[place], text_rs.at[back], column[place],
        )

    def send_image(place):
        back = PLANE_BACK[place]
        image_copies[back] = send(
            images.at[0:ROWS], images.at[image_rows(back)],
            image_ss.at[place], image_rs.at[back], plane[place],
        )

    def hand_text(place):
        pair_copies[place] = send(
            texts.at[pl.ds(text_rows(0, place), ROWS)], texts.at[pl.ds(text_rows(1, place), ROWS)],
            pair_ss.at[place], pair_rs.at[place], twin,
        )

    for place in range(1, 8):
        send_text(place)
        send_image(2 * place - 1)
        send_image(2 * place)
    send_image(15)
    hand_text(0)

    def tile(first, second, diagonal):
        rows = pl.ds(pl.multiple_of(first * GROUP, GROUP), GROUP)
        cols = pl.ds(pl.multiple_of(second * GROUP, GROUP), GROUP)
        products = lax.dot_general(
            images[rows, :], texts[cols, :], (((1,), (1,)), ((), ())),
            preferred_element_type=jnp.float32,
        )
        grown = jnp.exp2(products * temper2 + offset2)
        above = 1.0 + grown
        slope = grown / above
        packed = above[0:128] * above[128:256]
        packed = packed[0:64] * packed[64:128]
        packed = packed[0:32] * packed[32:64]
        loss = fold(jnp.log(packed))
        if diagonal:
            row = lax.broadcasted_iota(jnp.int32, (GROUP, GROUP), 0)
            col = lax.broadcasted_iota(jnp.int32, (GROUP, GROUP), 1)
            matched = jnp.where((row == col) & (row < ROWS), 1.0, 0.0)
            slope = slope - matched
            loss = loss - fold(matched * (products * temper + offset))
        sums[0] += loss
        sums[1] += fold(slope)
        sums[2] += fold(slope * products)
        slope = slope.astype(jnp.bfloat16)
        slopes[rows, cols] = slope
        slopes_t[cols, rows] = slope.T

    for step in range(4):
        for place in (2 * step, 2 * step + 1):
            if place:
                text_copies[place].wait_recv()
                hand_text(place)
        for place in range(4 * step, 4 * step + 4):
            if place:
                image_copies[place].wait_recv()
        for place in (2 * step, 2 * step + 1):
            pair_copies[place].wait_recv()
        if step == 0:
            tile(0, 0, True)
        else:

            def body(count, carry, step=step):
                tile(jnp.minimum(step, count), jnp.minimum(step, 2 * step - count), False)
                return carry

            lax.fori_loop(0, 2 * step + 1, body, 0)

    def spread(stage, values, peers):
        found_out[stage] = values
        return [
            send(found_out.at[stage], found_in.at[stage, n], f_ss.at[stage, n], f_rs.at[stage, n], peer)
            for n, peer in enumerate(peers)
        ]

    def collect(stage, values, copies):
        for n, copy in enumerate(copies):
            copy.wait_recv()
            values = values + found_in[stage, n]
        return values

    lane_sums = [jnp.sum(sums[n], keepdims=True) for n in range(3)]
    row = lax.broadcasted_iota(jnp.int32, (8, 128), 0)
    found = jnp.where(row == 0, lane_sums[0], jnp.where(row == 1, lane_sums[1], lane_sums[2]))
    found_copies = spread(0, found, plane[1:])

    gi_copies, gt_copies, gp_copies = {}, {}, {}
    temper3 = jnp.concatenate([temper] * 3, axis=1)

    def image_grads(group):
        rows = slice(group * GROUP, group * GROUP + GROUP)
        part = temper3 * jnp.dot(slopes[rows, :], texts[...], preferred_element_type=jnp.float32)
        image_part[rows, :] = part.astype(jnp.bfloat16)
        if group == 0:
            image_own[...] = part[0:ROWS]
        for place in range(4 * group, 4 * group + 4):
            if place:
                back = PLANE_BACK[place]
                gi_copies[back] = send(
                    image_part.at[image_rows(place)], image_in.at[back],
                    gi_ss.at[place], gi_rs.at[back], plane[place],
                )

    def text_grads(group):
        rows = slice(group * GROUP, group * GROUP + GROUP)
        part = temper3 * jnp.dot(slopes_t[rows, :], images[...], preferred_element_type=jnp.float32)
        own = slice(2 * group * ROWS, 2 * group * ROWS + 2 * ROWS)
        text_own[own, :] = part[0 : 2 * ROWS]
        pair_part[own, :] = part[2 * ROWS : 4 * ROWS].astype(jnp.bfloat16)
        gp_copies[group] = send(
            pair_part.at[own], pair_in.at[own], gp_ss.at[group], gp_rs.at[group], twin
        )

    def text_sums(group):
        gp_copies[group].wait_recv()
        for place in (2 * group + 1, 2 * group):
            own = slice(place * ROWS, place * ROWS + ROWS)
            part = text_own[own, :] + pair_in[own, :].astype(jnp.float32)
            if place == 0:
                text_own[own, :] = part
            else:
                back = COLUMN_BACK[place]
                text_part[own, :] = part.astype(jnp.bfloat16)
                gt_copies[back] = send(
                    text_part.at[own], text_in.at[back], gt_ss.at[place], gt_rs.at[back], column[place]
                )

    text_grads(3)
    image_grads(3)
    text_sums(3)
    text_grads(2)
    found = collect(0, found, found_copies)
    found_copies = spread(1, found, column[1:])
    image_grads(2)
    text_sums(2)
    text_grads(1)
    found = collect(1, found, found_copies)
    found_copies = spread(2, found, [twin])
    image_grads(1)
    text_sums(1)
    text_grads(0)
    image_grads(0)
    text_sums(0)

    found = collect(2, found, found_copies) * (1.0 / float(TOTAL) ** 2)
    scalars_ref[...] = jnp.where(row == 2, found * temper[:, 0:128], found)

    total = text_own[0:ROWS, :]
    for place in range(7, 0, -1):
        gt_copies[place].wait_recv()
        total = total + text_in[place].astype(jnp.float32)
    grad_text_ref[...] = back_rows(text_ref[...].astype(jnp.float32), total)

    total = image_own[...]
    for place in range(15, 0, -1):
        gi_copies[place].wait_recv()
        total = total + image_in[place].astype(jnp.float32)
    grad_image_ref[...] = back_rows(image_ref[...].astype(jnp.float32), total)

    for copy in started:
        copy.wait_send()


def local(image_emb, text_emb, log_temp, bias):
    bf16, f32 = jnp.bfloat16, jnp.float32
    vmem, smem = pl.BlockSpec(memory_space=pltpu.VMEM), pl.BlockSpec(memory_space=pltpu.SMEM)
    dma = pltpu.SemaphoreType.DMA
    grad_image, grad_text, scalars = pl.pallas_call(
        kernel,
        out_shape=(
            jax.ShapeDtypeStruct((ROWS, WIDTH), f32),
            jax.ShapeDtypeStruct((ROWS, WIDTH), f32),
            jax.ShapeDtypeStruct((8, 128), f32),
        ),
        in_specs=[vmem, vmem, smem, smem],
        out_specs=(vmem, vmem, vmem),
        scratch_shapes=[
            pltpu.VMEM((16 * ROWS, WIDTH), bf16),
            pltpu.VMEM((16 * ROWS, WIDTH), bf16),
            pltpu.VMEM((16 * ROWS, 16 * ROWS), bf16),
            pltpu.VMEM((16 * ROWS, 16 * ROWS), bf16),
            pltpu.VMEM((3, 8, 256), f32),
            pltpu.VMEM((16 * ROWS, WIDTH), bf16),
            pltpu.VMEM((8 * ROWS, WIDTH), bf16),
            pltpu.VMEM((8 * ROWS, WIDTH), bf16),
            pltpu.VMEM((ROWS, WIDTH), f32),
            pltpu.VMEM((8 * ROWS, WIDTH), f32),
            pltpu.VMEM((16, ROWS, WIDTH), bf16),
            pltpu.VMEM((8, ROWS, WIDTH), bf16),
            pltpu.VMEM((8 * ROWS, WIDTH), bf16),
            pltpu.VMEM((3, 15, 8, 128), f32),
            pltpu.VMEM((3, 8, 128), f32),
            dma((16,)), dma((16,)), dma((8,)), dma((8,)), dma((8,)), dma((8,)),
            dma((16,)), dma((16,)), dma((8,)), dma((8,)), dma((4,)), dma((4,)),
            dma((3, 15)), dma((3, 15)),
        ],
        compiler_params=pltpu.CompilerParams(
            collective_id=0, has_side_effects=True, vmem_limit_bytes=40 * 1024 * 1024
        ),
    )(image_emb, text_emb, log_temp, bias)
    return (scalars[0, 0:1], grad_image, grad_text, jnp.stack([scalars[2, 0], scalars[1, 0]]))


def solution(mesh):
    placed = (P(("blk", "narrow"), None), P(("blk", "narrow"), None), P(), P())
    return jax.shard_map(
        local,
        mesh=mesh,
        in_specs=placed,
        out_specs=(P(), P(("blk", "narrow"), None), P(("blk", "narrow"), None), P()),
        check_vma=False,
    )
```

time: 333 us -> 73.3 us (0.22)
  the two profiles are of different devices: /device:TPU:4 before, /device:TPU:1 now
where the time goes in v1:
time: 73.3 us; the launch traced here: 73.1 us
  Pallas kernels  65.6 us (89%)
  local copies, waits for them, and re-layouts  3.65 us (5%)
  between operations  1.94 us (3%)
  other arithmetic  1.88 us (3%)
    pallas_call x1, Pallas kernels, local(): pl.pallas_call(kernel, out_shape=(jax.ShapeDtypeStruct((ROWS, WIDTH), f32...  65.6 us
    unnamed x6, local copies, waits for them, and re-layouts  3.13 us
    another operation x1, other arithmetic, local(): jnp.stack([scalars[2, 0], scalars[1, 0]])  1.88 us

profile of v1, /device:TPU:1, one launch (start us, length us, event | category | flops | bytes accessed | tf_op | source)
XLA Modules:
  0.0 73.1 jit_solution(15360771570089085810)
XLA Ops:
  1.9 0.0 copy-start
  1.9 0.9 %copy-done = bf16[64,768]{1,0:T(8,128)(2,1)S(1)} copy-done((bf16[64,768]{1,0:T(8,128)(2,1)S(1)}, bf16[64,768]{1,0:T(8,128)(2,1)}, u32[]{:S(2)}) %copy-start) | copy-done | bytes 98328
  2.8 0.0 copy-start.1
  2.8 0.9 %copy-done.1 = bf16[64,768]{1,0:T(8,128)(2,1)S(1)} copy-done((bf16[64,768]{1,0:T(8,128)(2,1)S(1)}, bf16[64,768]{1,0:T(8,128)(2,1)}, u32[]{:S(2)}) %copy-start.1) | copy-done | bytes 98328
  3.7 65.6 %shard_map.75 = (f32[64,768]{1,0:T(8,128)S(1)}, f32[64,768]{1,0:T(8,128)S(1)}, f32[8,128]{1,0:T(8,128)S(1)}) custom-call(bf16[64,768]{1,0:T(8,128)(2,1)S(1)} %copy-done, bf16[64,768]{1,0:T(8,128)(2,1)S(1)} %copy-done.1, f32[1]{0:T(128)S(6)} %copy.10.temp_ref, f32[1]{0:T(128)S(6)} %copy.11.bias_ref), custom_call_target="tpu_custom_call" | custom-call | tf_op jit(solution)/shard_map/pallas_call | solution.py:275
  69.3 0.5 fusion
  69.9 1.9 %pad_maximum_fusion = f32[2]{0:T(128)} fusion(f32[1]{0:T(128)} %bitcast.2, f32[1]{0:T(128)} %bitcast.1), kind=kLoop, calls=%fused_computation | loop fusion | flops 2 | bytes 16 | tf_op jit(solution)/shard_map/stack | solution.py:308
  71.7 0.7 copy.12
  72.4 0.7 copy.13
Async XLA Ops:
  1.9 0.9 %copy-start = (bf16[64,768]{1,0:T(8,128)(2,1)S(1)}, bf16[64,768]{1,0:T(8,128)(2,1)}, u32[]{:S(2)}) copy-start(bf16[64,768]{1,0:T(8,128)(2,1)} %image_ref.1) | copy-start | bytes 294916
  2.8 0.9 %copy-start.1 = (bf16[64,768]{1,0:T(8,128)(2,1)S(1)}, bf16[64,768]{1,0:T(8,128)(2,1)}, u32[]{:S(2)}) copy-start(bf16[64,768]{1,0:T(8,128)(2,1)} %text_ref.1) | copy-start | bytes 294916

commit v2 on v1

v2 whole, which is shorter than its diff:
```python
import math

import jax
import jax.numpy as jnp
from jax import lax
from jax.experimental import pallas as pl
from jax.experimental.pallas import tpu as pltpu
from jax.sharding import PartitionSpec as P

MESH = pl.DeviceIdType.MESH
ROWS, WIDTH = 64, 768
HALF, LINE, GROUP = ROWS // 2, 2 * ROWS, 4 * ROWS
TOTAL = 16384
LOG2E = math.log2(math.e)

AROUND = (0, 1, 3, 2)
AROUND_BACK = tuple(AROUND.index(-d % 4) for d in AROUND)
COLUMN = (0, 1, 7, 6, 2, 4, 3, 5)
COLUMN_BACK = tuple(COLUMN.index(-d % 8) for d in COLUMN)


def image_row(half, line, place):
    return line * GROUP + half * LINE + place * HALF


def text_row(other, place):
    return (place // 2 * 4 + other * 2 + place % 2) * ROWS


def row_scale(values):
    return lax.rsqrt(jnp.sum(values * values, axis=-1, keepdims=True) + 1e-06)


def back_rows(values, upstream):
    inverse = row_scale(values)
    unit = values * inverse
    return inverse * (upstream - unit * jnp.sum(unit * upstream, axis=-1, keepdims=True))


def fold(values):
    return jnp.sum(jnp.reshape(values, (values.shape[0] // 8, 8, values.shape[1])), axis=0)


def wide(ref):
    return ref.astype(jnp.float32)


def kernel(
    image_hbm, text_hbm, temp_ref, bias_ref,
    grad_image_ref, grad_text_ref, scalars_ref,
    image_ref, text_ref, images, texts, slopes, slopes_t, sums,
    image_part, image_own, image_in, image_mid, image_last,
    text_part, text_own, text_in, pair_part, pair_in, text_mid, found_in, found_out,
    load, image_ss, image_rs, text_ss, text_rs, pair_ss, pair_rs,
    line_ss, line_rs, last_ss, last_rs, gt_ss, gt_rs, mid_ss, mid_rs, gp_ss, gp_rs, f_ss, f_rs,
):
    blk, narrow = lax.axis_index("blk"), lax.axis_index("narrow")
    x, core = lax.div(blk, 4), lax.rem(blk, 2)
    y = lax.rem(lax.div(blk, 2), 2) * 2 + lax.div(narrow, 8)
    z = lax.rem(narrow, 8)

    def device(dx, dy, dz, other):
        px, py, pz = lax.rem(x + dx, 4), lax.rem(y + dy, 4), lax.rem(z + dz, 8)
        pc = lax.rem(core + other, 2)
        return (px * 4 + lax.div(py, 2) * 2 + pc, lax.rem(py, 2) * 8 + pz)

    axes = ([device(d, 0, 0, 0) for d in AROUND], [device(0, d, 0, 0) for d in AROUND])
    column = {d: device(0, 0, d, 0) for d in range(1, 8)}
    twin = device(0, 0, 0, 1)

    barrier = pltpu.get_barrier_semaphore()
    peers = [axes[0][3], axes[1][3], *axes[0][1:3], *axes[1][1:3], *column.values(), twin]
    for peer in peers:
        pl.semaphore_signal(barrier, inc=1, device_id=peer, device_id_type=MESH)
    loads = [
        pltpu.make_async_copy(image_hbm, image_ref, load.at[0]),
        pltpu.make_async_copy(text_hbm, text_ref, load.at[1]),
    ]
    for copy in loads:
        copy.start()
    sums[...] = jnp.zeros_like(sums)
    temper = jnp.exp(jnp.full((1, 256), temp_ref[0], jnp.float32))
    offset = jnp.full((1, 256), bias_ref[0], jnp.float32)
    temper2, offset2 = temper * LOG2E, offset * LOG2E
    temper3 = jnp.concatenate([temper] * 3, axis=1)
    for copy in loads:
        copy.wait()
    image = wide(image_ref[...])
    image = (image * row_scale(image)).astype(jnp.bfloat16)
    for half in (0, 1):
        row = image_row(half, 0, 0)
        images[row : row + HALF, :] = image[half * HALF : half * HALF + HALF]
    text = wide(text_ref[...])
    texts[0:ROWS, :] = (text * row_scale(text)).astype(jnp.bfloat16)

    pl.semaphore_wait(barrier, len(peers))

    started = []

    def send(src, dst, send_sem, recv_sem, peer):
        copy = pltpu.make_async_remote_copy(
            src_ref=src, dst_ref=dst, send_sem=send_sem, recv_sem=recv_sem,
            device_id=peer, device_id_type=MESH,
        )
        copy.start()
        started.append(copy)
        return copy

    image_copies, text_copies, pair_copies = {}, {}, {}

    def first_image(half, place):
        back = AROUND_BACK[place]
        image_copies[half, 0, back] = send(
            images.at[pl.ds(image_row(half, 0, 0), HALF)],
            images.at[pl.ds(image_row(half, 0, back), HALF)],
            image_ss.at[half, 0, place], image_rs.at[half, 0, back], axes[half][place],
        )

    def pass_image(half, place):
        for line in (3, 1, 2):
            back = AROUND_BACK[line]
            image_copies[half, back, place] = send(
                images.at[pl.ds(image_row(half, 0, place), HALF)],
                images.at[pl.ds(image_row(half, back, place), HALF)],
                image_ss.at[half, line, place], image_rs.at[half, back, place], axes[1 - half][line],
            )

    def send_text(block, step, first, count, slot):
        source, target = text_row(0, COLUMN.index(block)), text_row(0, COLUMN.index((block - step) % 8))
        text_copies[(block - step) % 8, first] = send(
            texts.at[pl.ds(source + first, count)], texts.at[pl.ds(target + first, count)],
            text_ss.at[slot], text_rs.at[slot], column[step % 8],
        )

    def hand_text(block):
        place = COLUMN.index(block)
        pair_copies[block] = send(
            texts.at[pl.ds(text_row(0, place), ROWS)], texts.at[pl.ds(text_row(1, place), ROWS)],
            pair_ss.at[place], pair_rs.at[place], twin,
        )

    send_text(0, 2, 0, ROWS, 0)
    send_text(0, -2, 0, ROWS, 1)
    for place in (3, 1, 2):
        for half in (0, 1):
            first_image(half, place)
    send_text(0, 1, 0, ROWS, 2)
    send_text(0, -1, 0, ROWS, 3)
    hand_text(0)
    for half in (0, 1):
        pass_image(half, 0)
    for place in (1, 2, 3):
        for half in (0, 1):
            image_copies[half, 0, place].wait_recv()
            pass_image(half, place)
    text_copies[2, 0].wait_recv()
    send_text(2, -1, 0, ROWS, 4)
    send_text(2, -2, 0, HALF, 5)
    text_copies[6, 0].wait_recv()
    send_text(6, 1, 0, ROWS, 6)
    send_text(6, 2, HALF, HALF, 7)
    hand_text(2)
    hand_text(6)

    def tile(first, second, diagonal):
        rows = pl.ds(pl.multiple_of(first * GROUP, GROUP), GROUP)
        cols = pl.ds(pl.multiple_of(second * GROUP, GROUP), GROUP)
        products = lax.dot_general(
            images[rows, :], texts[cols, :], (((1,), (1,)), ((), ())),
            preferred_element_type=jnp.float32,
        )
        grown = jnp.exp2(products * temper2 + offset2)
        above = 1.0 + grown
        slope = grown / above
        packed = above[0:128] * above[128:256]
        packed = packed[0:64] * packed[64:128]
        packed = packed[0:32] * packed[32:64]
        loss = fold(jnp.log(packed))
        if diagonal:
            row = lax.broadcasted_iota(jnp.int32, (GROUP, GROUP), 0)
            col = lax.broadcasted_iota(jnp.int32, (GROUP, GROUP), 1)
            upper = (row == col) & (row < HALF)
            lower = (row - LINE + HALF == col) & (row >= LINE) & (row < LINE + HALF)
            matched = jnp.where(upper | lower, 1.0, 0.0)
            slope = slope - matched
            loss = loss - fold(matched * (products * temper + offset))
        sums[0] += loss
        sums[1] += fold(slope)
        sums[2] += fold(slope * products)
        slope = slope.astype(jnp.bfloat16)
        slopes[rows, cols] = slope
        slopes_t[cols, rows] = slope.T

    def tiles(firsts, seconds):
        count = seconds[1] - seconds[0]

        def body(n, carry):
            tile(firsts[0] + lax.div(n, count), seconds[0] + lax.rem(n, count), False)
            return carry

        lax.fori_loop(0, (firsts[1] - firsts[0]) * count, body, 0)

    def wait_lines(line):
        for half in (0, 1):
            for place in range(4):
                image_copies[half, line, place].wait_recv()

    for block in (1, 7):
        text_copies[block, 0].wait_recv()
        hand_text(block)
    for block in (0, 1):
        pair_copies[block].wait_recv()
    tile(0, 0, True)
    for block in (6, 7):
        pair_copies[block].wait_recv()
    tiles((0, 1), (1, 2))
    wait_lines(1)
    wait_lines(2)
    tiles((1, 3), (0, 2))
    for block in (3, 5):
        text_copies[block, 0].wait_recv()
        hand_text(block)
    wait_lines(3)
    tiles((3, 4), (0, 2))
    for first in (0, HALF):
        text_copies[4, first].wait_recv()
    hand_text(4)
    for block in (3, 5):
        pair_copies[block].wait_recv()
    tiles((0, 4), (3, 4))
    for block in (2, 4):
        pair_copies[block].wait_recv()
    tiles((0, 4), (2, 3))

    def spread(stage, values, peers):
        found_out[stage] = values
        return [
            send(found_out.at[stage], found_in.at[stage, n], f_ss.at[stage, n], f_rs.at[stage, n], peer)
            for n, peer in enumerate(peers)
        ]

    def collect(stage, values, copies):
        for n, copy in enumerate(copies):
            copy.wait_recv()
            values = values + found_in[stage, n]
        return values

    lane_sums = [jnp.sum(sums[n], keepdims=True) for n in range(3)]
    row = lax.broadcasted_iota(jnp.int32, (8, 128), 0)
    found = jnp.where(row == 0, lane_sums[0], jnp.where(row == 1, lane_sums[1], lane_sums[2]))
    found_copies = spread(0, found, axes[0][1:])

    line_copies, last_copies, gt_copies, mid_copies, gp_copies = {}, {}, {}, {}, {}

    def image_grads(line):
        rows = slice(line * GROUP, line * GROUP + GROUP)
        part = temper3 * jnp.dot(slopes[rows, :], texts[...], preferred_element_type=jnp.float32)
        if line == 0:
            image_own[...] = part
        else:
            image_part[rows, :] = part.astype(jnp.bfloat16)

    def send_lines(line, own):
        first, count = (0, HALF) if own else (HALF, LINE - HALF)
        back = AROUND_BACK[line]
        for half in (0, 1):
            line_copies[half, back, own] = send(
                image_part.at[pl.ds(image_row(half, line, 0) + first, count)],
                image_in.at[half, back, pl.ds(first, count)],
                line_ss.at[half, line, own], line_rs.at[half, back, own], axes[1 - half][line],
            )

    def line_sum(half, own):
        first, count = (0, HALF) if own else (HALF, LINE - HALF)
        row = half * LINE + first
        part = image_own[row : row + count, :]
        for line in (3, 1, 2):
            line_copies[half, line, own].wait_recv()
            part = part + wide(image_in[half, line, first : first + count, :])
        return part

    def text_grads(group):
        rows = slice(group * GROUP, group * GROUP + GROUP)
        part = temper3 * jnp.dot(slopes_t[rows, :], images[...], preferred_element_type=jnp.float32)
        own = slice(group * LINE, group * LINE + LINE)
        text_own[own, :] = part[0:LINE]
        pair_part[own, :] = part[LINE:GROUP].astype(jnp.bfloat16)
        gp_copies[group] = send(
            pair_part.at[own], pair_in.at[own], gp_ss.at[group], gp_rs.at[group], twin
        )

    def own_rows(block, first=0, count=ROWS):
        place = COLUMN.index(block)
        return slice(place * ROWS + first, place * ROWS + first + count)

    def text_sums(group):
        gp_copies[group].wait_recv()
        own = slice(group * LINE, group * LINE + LINE)
        part = text_own[own, :] + wide(pair_in[own, :])
        text_own[own, :] = part
        text_part[own, :] = part.astype(jnp.bfloat16)

    def send_mid(block, step, first, count, slot):
        mid_copies[slot] = send(
            text_part.at[own_rows(block, first, count)], text_mid.at[slot, pl.ds(first, count)],
            mid_ss.at[slot], mid_rs.at[slot], column[step % 8],
        )

    def send_share(block, slot):
        gt_copies[slot] = send(
            text_part.at[own_rows(block)], text_in.at[slot], gt_ss.at[slot], gt_rs.at[slot], column[block]
        )

    def add_mid(block, near, far, first, slot):
        mid_copies[near].wait_recv()
        part = text_own[own_rows(block), :] + wide(text_mid[near])
        mid_copies[far].wait_recv()
        more = part[first : first + HALF] + wide(text_mid[far, first : first + HALF, :])
        part = jnp.concatenate([more, part[HALF:]] if first == 0 else [part[:HALF], more], axis=0)
        text_part[own_rows(block), :] = part.astype(jnp.bfloat16)
        send_share(block, slot)

    text_grads(3)
    image_grads(3)
    send_lines(3, 0)
    send_lines(3, 1)
    text_sums(3)
    send_mid(3, 1, 0, ROWS, 0)
    send_mid(5, -1, 0, ROWS, 1)
    text_grads(2)
    image_grads(1)
    send_lines(1, 0)
    text_sums(2)
    send_mid(4, 2, 0, HALF, 2)
    send_mid(4, -2, HALF, HALF, 3)
    text_grads(1)
    image_grads(2)
    send_lines(2, 0)
    send_lines(1, 1)
    send_lines(2, 1)
    text_sums(1)
    send_share(7, 0)
    found = collect(0, found, found_copies)
    found_copies = spread(1, found, axes[1][1:])
    text_grads(0)
    image_grads(0)
    text_sums(0)
    send_share(1, 1)
    add_mid(2, 0, 2, 0, 2)
    add_mid(6, 1, 3, HALF, 3)
    found = collect(1, found, found_copies)
    found_copies = spread(2, found, list(column.values()))

    for half in (0, 1):
        part = line_sum(half, 0).astype(jnp.bfloat16)
        image_mid[half] = part
        for place in (3, 1, 2):
            back = AROUND_BACK[place]
            last_copies[half, back] = send(
                image_mid.at[half, pl.ds(place * HALF - HALF, HALF)], image_last.at[half, back],
                last_ss.at[half, place], last_rs.at[half, back], axes[half][place],
            )
    found = collect(2, found, found_copies)
    found_copies = spread(3, found, [twin])
    ends = [line_sum(half, 1) for half in (0, 1)]

    total = text_own[0:ROWS, :]
    for slot in range(4):
        gt_copies[slot].wait_recv()
        total = total + wide(text_in[slot])
    grad_text_ref[...] = back_rows(wide(text_ref[...]), total)

    found = collect(3, found, found_copies) * (1.0 / float(TOTAL) ** 2)
    scalars_ref[...] = jnp.where(row == 2, found * temper[:, 0:128], found)

    for half in (0, 1):
        total = ends[half]
        for place in (1, 2, 3):
            last_copies[half, place].wait_recv()
            total = total + wide(image_last[half, place])
        rows = slice(half * HALF, half * HALF + HALF)
        grad_image_ref[rows, :] = back_rows(wide(image_ref[rows, :]), total)

    for copy in started:
        copy.wait_send()


def local(image_emb, text_emb, log_temp, bias):
    bf16, f32 = jnp.bfloat16, jnp.float32
    vmem, smem = pl.BlockSpec(memory_space=pltpu.VMEM), pl.BlockSpec(memory_space=pltpu.SMEM)
    hbm = pl.BlockSpec(memory_space=pl.ANY)
    dma = pltpu.SemaphoreType.DMA
    grad_image, grad_text, scalars = pl.pallas_call(
        kernel,
        out_shape=(
            jax.ShapeDtypeStruct((ROWS, WIDTH), f32),
            jax.ShapeDtypeStruct((ROWS, WIDTH), f32),
            jax.ShapeDtypeStruct((8, 128), f32),
        ),
        in_specs=[hbm, hbm, smem, smem],
        out_specs=(vmem, vmem, vmem),
        scratch_shapes=[
            pltpu.VMEM((ROWS, WIDTH), bf16),
            pltpu.VMEM((ROWS, WIDTH), bf16),
            pltpu.VMEM((16 * ROWS, WIDTH), bf16),
            pltpu.VMEM((16 * ROWS, WIDTH), bf16),
            pltpu.VMEM((16 * ROWS, 16 * ROWS), bf16),
            pltpu.VMEM((16 * ROWS, 16 * ROWS), bf16),
            pltpu.VMEM((3, 8, 256), f32),
            pltpu.VMEM((16 * ROWS, WIDTH), bf16),
            pltpu.VMEM((GROUP, WIDTH), f32),
            pltpu.VMEM((2, 4, LINE, WIDTH), bf16),
            pltpu.VMEM((2, LINE - HALF, WIDTH), bf16),
            pltpu.VMEM((2, 4, HALF, WIDTH), bf16),
            pltpu.VMEM((8 * ROWS, WIDTH), bf16),
            pltpu.VMEM((8 * ROWS, WIDTH), f32),
            pltpu.VMEM((4, ROWS, WIDTH), bf16),
            pltpu.VMEM((8 * ROWS, WIDTH), bf16),
            pltpu.VMEM((8 * ROWS, WIDTH), bf16),
            pltpu.VMEM((4, ROWS, WIDTH), bf16),
            pltpu.VMEM((4, 7, 8, 128), f32),
            pltpu.VMEM((4, 8, 128), f32),
            dma((2,)),
            dma((2, 4, 4)), dma((2, 4, 4)), dma((8,)), dma((8,)), dma((8,)), dma((8,)),
            dma((2, 4, 2)), dma((2, 4, 2)), dma((2, 4)), dma((2, 4)),
            dma((4,)), dma((4,)), dma((4,)), dma((4,)), dma((4,)), dma((4,)),
            dma((4, 7)), dma((4, 7)),
        ],
        compiler_params=pltpu.CompilerParams(
            collective_id=0, has_side_effects=True, vmem_limit_bytes=56 * 1024 * 1024
        ),
    )(image_emb, text_emb, log_temp, bias)
    return (scalars[0, 0:1], grad_image, grad_text, jnp.stack([scalars[2, 0], scalars[1, 0]]))


def solution(mesh):
    placed = (P(("blk", "narrow"), None), P(("blk", "narrow"), None), P(), P())
    return jax.shard_map(
        local,
        mesh=mesh,
        in_specs=placed,
        out_specs=(P(), P(("blk", "narrow"), None), P(("blk", "narrow"), None), P()),
        check_vma=False,
    )
```

time: 73.3 us -> 59.6 us (0.81)
  Pallas kernels: 65.6 us -> 52 us
    pallas_call x1, Pallas kernels: 65.6 us -> 52 us  [local(): pl.pallas_call(kernel, out_shape=(jax.ShapeDtypeStruct((ROWS, WIDTH), f32...]
    slice x1, local copies, waits for them, and re-layouts: 0.52 us -> 1.32 us  [local(): scalars[2, 0]]
    unnamed x6 -> x4, local copies, waits for them, and re-layouts: 3.13 us -> 2.34 us
where the time goes in v2:
time: 59.6 us; the launch traced here: 59.4 us
  Pallas kernels  52 us (87%)
  local copies, waits for them, and re-layouts  3.65 us (6%)
  between operations  1.93 us (3%)
  other arithmetic  1.88 us (3%)
    pallas_call x1, Pallas kernels, local(): pl.pallas_call(kernel, out_shape=(jax.ShapeDtypeStruct((ROWS, WIDTH), f32...  52 us
    unnamed x4, local copies, waits for them, and re-layouts  2.34 us
    another operation x1, other arithmetic, local(): jnp.stack([scalars[2, 0], scalars[1, 0]])  1.88 us
    slice x1, local copies, waits for them, and re-layouts, local(): scalars[2, 0]  1.32 us

profile of v2, /device:TPU:1, one launch (start us, length us, event | category | flops | bytes accessed | tf_op | source)
XLA Modules:
  0.0 59.4 jit_solution(14670337206210418461)
XLA Ops:
  1.9 52.0 %shard_map.75 = (f32[64,768]{1,0:T(8,128)}, f32[64,768]{1,0:T(8,128)}, f32[8,128]{1,0:T(8,128)}) custom-call(bf16[64,768]{1,0:T(8,128)(2,1)} %image_hbm.1, bf16[64,768]{1,0:T(8,128)(2,1)} %text_hbm.1, f32[1]{0:T(128)S(6)} %copy.10.temp_ref, f32[1]{0:T(128)S(6)} %copy.11.bias_ref), custom_call_target="tpu_custom_call" | custom-call | tf_op jit(solution)/shard_map/pallas_call | solution.py:393
  53.9 1.3 %fusion = (f32[1,1]{1,0:T(1,128)}, f32[1,1]{1,0:T(1,128)}, f32[1,1]{1,0:T(1,128)}) fusion(f32[8,128]{1,0:T(8,128)} %get-tuple-element.7), kind=kLoop, calls=%fused_computation.1 | loop fusion | bytes 24 | tf_op jit(solution)/shard_map/slice | solution.py:433
  55.2 1.9 %pad_maximum_fusion = f32[2]{0:T(128)} fusion(f32[1]{0:T(128)} %bitcast.2, f32[1]{0:T(128)} %bitcast.1), kind=kLoop, calls=%fused_computation | loop fusion | flops 2 | bytes 16 | tf_op jit(solution)/shard_map/stack | solution.py:433
  57.1 0.0 copy-start
  57.1 1.7 %copy.12 = f32[64,768]{1,0:T(8,128)} copy(f32[64,768]{1,0:T(8,128)} %get-tuple-element.18) | data formatting | bytes 393216
  58.7 0.0 copy-done
  58.7 0.7 %copy.13 = f32[64,768]{1,0:T(8,128)} copy(f32[64,768]{1,0:T(8,128)S(1)} %copy-done) | data formatting | bytes 393216
Async XLA Ops:
  57.1 1.7 %copy-start = (f32[64,768]{1,0:T(8,128)S(1)}, f32[64,768]{1,0:T(8,128)}, u32[]{:S(2)}) copy-start(f32[64,768]{1,0:T(8,128)} %get-tuple-element.19) | copy-start | bytes 589828

commit v3 on v2

--- a/solution.py
+++ b/solution.py
@@ -46,9 +46,9 @@
 
 
 def kernel(
-    image_hbm, text_hbm, temp_ref, bias_ref,
-    grad_image_ref, grad_text_ref, scalars_ref,
-    image_ref, text_ref, images, texts, slopes, slopes_t, sums,
+    image_hbm, text_hbm, temp_hbm, bias_hbm,
+    total_image_ref, total_text_ref, scalars_ref,
+    temp_ref, bias_ref, image_ref, text_ref, images, texts, texts_t, slopes, slopes_t, sums,
     image_part, image_own, image_in, image_mid, image_last,
     text_part, text_own, text_in, pair_part, pair_in, text_mid, found_in, found_out,
     load, image_ss, image_rs, text_ss, text_rs, pair_ss, pair_rs,
@@ -75,16 +75,18 @@
     loads = [
         pltpu.make_async_copy(image_hbm, image_ref, load.at[0]),
         pltpu.make_async_copy(text_hbm, text_ref, load.at[1]),
+        pltpu.make_async_copy(temp_hbm, temp_ref, load.at[2]),
+        pltpu.make_async_copy(bias_hbm, bias_ref, load.at[3]),
     ]
     for copy in loads:
         copy.start()
     sums[...] = jnp.zeros_like(sums)
+    for copy in loads:
+        copy.wait()
     temper = jnp.exp(jnp.full((1, 256), temp_ref[0], jnp.float32))
     offset = jnp.full((1, 256), bias_ref[0], jnp.float32)
     temper2, offset2 = temper * LOG2E, offset * LOG2E
     temper3 = jnp.concatenate([temper] * 3, axis=1)
-    for copy in loads:
-        copy.wait()
     image = wide(image_ref[...])
     image = (image * row_scale(image)).astype(jnp.bfloat16)
     for half in (0, 1):
@@ -162,13 +164,9 @@
     hand_text(2)
     hand_text(6)
 
-    def tile(first, second, diagonal):
-        rows = pl.ds(pl.multiple_of(first * GROUP, GROUP), GROUP)
-        cols = pl.ds(pl.multiple_of(second * GROUP, GROUP), GROUP)
-        products = lax.dot_general(
-            images[rows, :], texts[cols, :], (((1,), (1,)), ((), ())),
-            preferred_element_type=jnp.float32,
-        )
+    def pairs(products, first, second):
+        rows = slice(first * GROUP, first * GROUP + GROUP)
+        cols = slice(second * GROUP, second * GROUP + GROUP)
         grown = jnp.exp2(products * temper2 + offset2)
         above = 1.0 + grown
         slope = grown / above
@@ -176,7 +174,7 @@
         packed = packed[0:64] * packed[64:128]
         packed = packed[0:32] * packed[32:64]
         loss = fold(jnp.log(packed))
-        if diagonal:
+        if first == 0 and second == 0:
             row = lax.broadcasted_iota(jnp.int32, (GROUP, GROUP), 0)
             col = lax.broadcasted_iota(jnp.int32, (GROUP, GROUP), 1)
             upper = (row == col) & (row < HALF)
@@ -184,53 +182,34 @@
             matched = jnp.where(upper | lower, 1.0, 0.0)
             slope = slope - matched
             loss = loss - fold(matched * (products * temper + offset))
-        sums[0] += loss
-        sums[1] += fold(slope)
-        sums[2] += fold(slope * products)
-        slope = slope.astype(jnp.bfloat16)
-        slopes[rows, cols] = slope
-        slopes_t[cols, rows] = slope.T
-
-    def tiles(firsts, seconds):
-        count = seconds[1] - seconds[0]
-
-        def body(n, carry):
-            tile(firsts[0] + lax.div(n, count), seconds[0] + lax.rem(n, count), False)
-            return carry
-
-        lax.fori_loop(0, (firsts[1] - firsts[0]) * count, body, 0)
+        slope_b = slope.astype(jnp.bfloat16)
+        slopes[rows, cols] = slope_b
+        slopes_t[cols, rows] = slope_b.T
+        return loss, fold(slope), fold(slope * products)
+
+    def tiles(*places):
+        products = [
+            jnp.dot(
+                images[first * GROUP : first * GROUP + GROUP, :],
+                texts_t[:, second * GROUP : second * GROUP + GROUP],
+                preferred_element_type=jnp.float32,
+            )
+            for first, second in places
+        ]
+        shares = [pairs(product, *place) for product, place in zip(products, places)]
+        for n in range(3):
+            sums[n] += sum(share[n] for share in shares)
 
     def wait_lines(line):
         for half in (0, 1):
             for place in range(4):
                 image_copies[half, line, place].wait_recv()
 
-    for block in (1, 7):
-        text_copies[block, 0].wait_recv()
-        hand_text(block)
-    for block in (0, 1):
-        pair_copies[block].wait_recv()
-    tile(0, 0, True)
-    for block in (6, 7):
-        pair_copies[block].wait_recv()
-    tiles((0, 1), (1, 2))
-    wait_lines(1)
-    wait_lines(2)
-    tiles((1, 3), (0, 2))
-    for block in (3, 5):
-        text_copies[block, 0].wait_recv()
-        hand_text(block)
-    wait_lines(3)
-    tiles((3, 4), (0, 2))
-    for first in (0, HALF):
-        text_copies[4, first].wait_recv()
-    hand_text(4)
-    for block in (3, 5):
-        pair_copies[block].wait_recv()
-    tiles((0, 4), (3, 4))
-    for block in (2, 4):
-        pair_copies[block].wait_recv()
-    tiles((0, 4), (2, 3))
+    def turn_texts(group):
+        for block in COLUMN[2 * group : 2 * group + 2]:
+            pair_copies[block].wait_recv()
+        rows = slice(group * GROUP, group * GROUP + GROUP)
+        texts_t[:, rows] = texts[rows, :].T
 
     def spread(stage, values, peers):
         found_out[stage] = values
@@ -245,11 +224,7 @@
             values = values + found_in[stage, n]
         return values
 
-    lane_sums = [jnp.sum(sums[n], keepdims=True) for n in range(3)]
     row = lax.broadcasted_iota(jnp.int32, (8, 128), 0)
-    found = jnp.where(row == 0, lane_sums[0], jnp.where(row == 1, lane_sums[1], lane_sums[2]))
-    found_copies = spread(0, found, axes[0][1:])
-
     line_copies, last_copies, gt_copies, mid_copies, gp_copies = {}, {}, {}, {}, {}
 
     def image_grads(line):
@@ -320,40 +295,64 @@
         text_part[own_rows(block), :] = part.astype(jnp.bfloat16)
         send_share(block, slot)
 
-    text_grads(3)
+    for block in (1, 7):
+        text_copies[block, 0].wait_recv()
+        hand_text(block)
+    turn_texts(0)
+    turn_texts(1)
+    tiles((0, 0), (0, 1))
+    wait_lines(1)
+    wait_lines(2)
+    tiles((1, 0), (1, 1), (2, 0), (2, 1))
+    for block in (3, 5):
+        text_copies[block, 0].wait_recv()
+        hand_text(block)
+    wait_lines(3)
+    tiles((3, 0), (3, 1))
+    for first in (0, HALF):
+        text_copies[4, first].wait_recv()
+    hand_text(4)
+    turn_texts(3)
+    tiles((3, 3), (1, 3), (2, 3), (0, 3))
+    turn_texts(2)
+    tiles((3, 2), (1, 2), (2, 2), (0, 2))
+
+    lane_sums = [jnp.sum(sums[n], keepdims=True) for n in range(3)]
+    found = jnp.where(row == 0, lane_sums[0], jnp.where(row == 1, lane_sums[1], lane_sums[2]))
+    found_copies = spread(0, found, [twin])
     image_grads(3)
     send_lines(3, 0)
     send_lines(3, 1)
+    text_grads(3)
+    image_grads(1)
+    send_lines(1, 0)
+    found = collect(0, found, found_copies)
+    found_copies = spread(1, found, list(column.values()))
+    text_grads(2)
     text_sums(3)
     send_mid(3, 1, 0, ROWS, 0)
     send_mid(5, -1, 0, ROWS, 1)
-    text_grads(2)
-    image_grads(1)
-    send_lines(1, 0)
+    image_grads(2)
+    send_lines(2, 0)
+    send_lines(1, 1)
+    send_lines(2, 1)
     text_sums(2)
     send_mid(4, 2, 0, HALF, 2)
     send_mid(4, -2, HALF, HALF, 3)
     text_grads(1)
-    image_grads(2)
-    send_lines(2, 0)
-    send_lines(1, 1)
-    send_lines(2, 1)
+    text_grads(0)
+    image_grads(0)
     text_sums(1)
     send_share(7, 0)
-    found = collect(0, found, found_copies)
-    found_copies = spread(1, found, axes[1][1:])
-    text_grads(0)
-    image_grads(0)
     text_sums(0)
     send_share(1, 1)
+    found = collect(1, found, found_copies)
+    found_copies = spread(2, found, axes[1][1:])
     add_mid(2, 0, 2, 0, 2)
     add_mid(6, 1, 3, HALF, 3)
-    found = collect(1, found, found_copies)
-    found_copies = spread(2, found, list(column.values()))
 
     for half in (0, 1):
-        part = line_sum(half, 0).astype(jnp.bfloat16)
-        image_mid[half] = part
+        image_mid[half] = line_sum(half, 0).astype(jnp.bfloat16)
         for place in (3, 1, 2):
             back = AROUND_BACK[place]
             last_copies[half, back] = send(
@@ -361,17 +360,14 @@
                 last_ss.at[half, place], last_rs.at[half, back], axes[half][place],
             )
     found = collect(2, found, found_copies)
-    found_copies = spread(3, found, [twin])
+    found_copies = spread(3, found, axes[0][1:])
     ends = [line_sum(half, 1) for half in (0, 1)]
 
     total = text_own[0:ROWS, :]
     for slot in range(4):
         gt_copies[slot].wait_recv()
         total = total + wide(text_in[slot])
-    grad_text_ref[...] = back_rows(wide(text_ref[...]), total)
-
-    found = collect(3, found, found_copies) * (1.0 / float(TOTAL) ** 2)
-    scalars_ref[...] = jnp.where(row == 2, found * temper[:, 0:128], found)
+    total_text_ref[...] = total
 
     for half in (0, 1):
         total = ends[half]
@@ -379,31 +375,45 @@
             last_copies[half, place].wait_recv()
             total = total + wide(image_last[half, place])
         rows = slice(half * HALF, half * HALF + HALF)
-        grad_image_ref[rows, :] = back_rows(wide(image_ref[rows, :]), total)
+        total_image_ref[rows, :] = total
+
+    found = collect(3, found, found_copies) * (1.0 / float(TOTAL) ** 2)
+    lane = lax.broadcasted_iota(jnp.int32, (8, 128), 1)
+    scale, slope = found[2:3] * temper[:, 0:128], found[1:2]
+    scalars_ref[...] = jnp.where(row == 0, found, jnp.where(lane == 0, scale, slope))
 
     for copy in started:
         copy.wait_send()
 
 
+def finish(image_ref, text_ref, total_image_ref, total_text_ref, scalars_ref, mean_ref, grad_image_ref, grad_text_ref, pair_ref):
+    grad_image_ref[...] = back_rows(wide(image_ref[...]), total_image_ref[...])
+    grad_text_ref[...] = back_rows(wide(text_ref[...]), total_text_ref[...])
+    mean_ref[...] = scalars_ref[0, 0:1]
+    pair_ref[...] = scalars_ref[1, 0:2]
+
+
 def local(image_emb, text_emb, log_temp, bias):
     bf16, f32 = jnp.bfloat16, jnp.float32
-    vmem, smem = pl.BlockSpec(memory_space=pltpu.VMEM), pl.BlockSpec(memory_space=pltpu.SMEM)
-    hbm = pl.BlockSpec(memory_space=pl.ANY)
+    vmem, hbm = pl.BlockSpec(memory_space=pltpu.VMEM), pl.BlockSpec(memory_space=pltpu.HBM)
     dma = pltpu.SemaphoreType.DMA
-    grad_image, grad_text, scalars = pl.pallas_call(
+    total_image, total_text, scalars = pl.pallas_call(
         kernel,
         out_shape=(
             jax.ShapeDtypeStruct((ROWS, WIDTH), f32),
             jax.ShapeDtypeStruct((ROWS, WIDTH), f32),
             jax.ShapeDtypeStruct((8, 128), f32),
         ),
-        in_specs=[hbm, hbm, smem, smem],
+        in_specs=[hbm] * 4,
         out_specs=(vmem, vmem, vmem),
         scratch_shapes=[
+            pltpu.SMEM((1,), f32),
+            pltpu.SMEM((1,), f32),
             pltpu.VMEM((ROWS, WIDTH), bf16),
             pltpu.VMEM((ROWS, WIDTH), bf16),
             pltpu.VMEM((16 * ROWS, WIDTH), bf16),
             pltpu.VMEM((16 * ROWS, WIDTH), bf16),
+            pltpu.VMEM((WIDTH, 16 * ROWS), bf16),
             pltpu.VMEM((16 * ROWS, 16 * ROWS), bf16),
             pltpu.VMEM((16 * ROWS, 16 * ROWS), bf16),
             pltpu.VMEM((3, 8, 256), f32),
@@ -420,7 +430,7 @@
             pltpu.VMEM((4, ROWS, WIDTH), bf16),
             pltpu.VMEM((4, 7, 8, 128), f32),
             pltpu.VMEM((4, 8, 128), f32),
-            dma((2,)),
+            dma((4,)),
             dma((2, 4, 4)), dma((2, 4, 4)), dma((8,)), dma((8,)), dma((8,)), dma((8,)),
             dma((2, 4, 2)), dma((2, 4, 2)), dma((2, 4)), dma((2, 4)),
             dma((4,)), dma((4,)), dma((4,)), dma((4,)), dma((4,)), dma((4,)),
@@ -430,7 +440,18 @@
             collective_id=0, has_side_effects=True, vmem_limit_bytes=56 * 1024 * 1024
         ),
     )(image_emb, text_emb, log_temp, bias)
-    return (scalars[0, 0:1], grad_image, grad_text, jnp.stack([scalars[2, 0], scalars[1, 0]]))
+    mean_loss, grad_image, grad_text, scalar_grads = pl.pallas_call(
+        finish,
+        out_shape=(
+            jax.ShapeDtypeStruct((1,), f32),
+            jax.ShapeDtypeStruct((ROWS, WIDTH), f32),
+            jax.ShapeDtypeStruct((ROWS, WIDTH), f32),
+            jax.ShapeDtypeStruct((2,), f32),
+        ),
+        in_specs=[vmem] * 5,
+        out_specs=(vmem,) * 4,
+    )(image_emb, text_emb, total_image, total_text, scalars)
+    return (mean_loss, grad_image, grad_text, scalar_grads)
 
 
 def solution(mesh):

time: 59.6 us -> 49.9 us (0.84)
  Pallas kernels: 52 us -> 47.8 us
  local copies, waits for them, and re-layouts: 3.65 us -> 0 us
  other arithmetic: 1.88 us -> 0 us
    pallas_call x1, Pallas kernels: 52 us -> 45.8 us  [local(): pl.pallas_call(kernel, out_shape=(jax.ShapeDtypeStruct((ROWS, WIDTH), f32...]
    unnamed x4 -> x0, local copies, waits for them, and re-layouts: 2.34 us -> none
    pallas_call x0 -> x1, Pallas kernels: none -> 2.06 us  [local(): pl.pallas_call(finish, out_shape=(jax.ShapeDtypeStruct((1,), f32), jax.Sh...]
    another operation x1 -> x0, other arithmetic: 1.88 us -> none  [local(): jnp.stack([scalars[2, 0], scalars[1, 0]])]
    slice x1 -> x0, local copies, waits for them, and re-layouts: 1.32 us -> none  [local(): scalars[2, 0]]
where the time goes in v3:
time: 49.9 us; the launch traced here: 49.7 us
  Pallas kernels  47.8 us (96%)
  between operations  1.93 us (4%)
    pallas_call x1, Pallas kernels, local(): pl.pallas_call(kernel, out_shape=(jax.ShapeDtypeStruct((ROWS, WIDTH), f32...  45.8 us
    pallas_call x1, Pallas kernels, local(): pl.pallas_call(finish, out_shape=(jax.ShapeDtypeStruct((1,), f32), jax.Sh...  2.06 us

profile of v3, /device:TPU:1, one launch (start us, length us, event | category | flops | bytes accessed | tf_op | source)
XLA Modules:
  0.0 49.7 jit_solution(12177367706997981650)
XLA Ops:
  1.9 45.8 %shard_map.75 = (f32[64,768]{1,0:T(8,128)}, f32[64,768]{1,0:T(8,128)}, f32[8,128]{1,0:T(8,128)}) custom-call(bf16[64,768]{1,0:T(8,128)(2,1)} %image_ref.1, bf16[64,768]{1,0:T(8,128)(2,1)} %text_ref.1, f32[1]{0:T(128)S(6)} %copy.8.temp_hbm, f32[1]{0:T(128)S(6)} %copy.9.bias_hbm), custom_call_target="tpu_custom_call" | custom-call | tf_op jit(solution)/shard_map/pallas_call | solution.py:400
  47.7 2.1 %shard_map.76 = (f32[1]{0:T(128)}, f32[64,768]{1,0:T(8,128)}, f32[64,768]{1,0:T(8,128)}, f32[2]{0:T(128)}) custom-call(bf16[64,768]{1,0:T(8,128)(2,1)} %image_ref.1, bf16[64,768]{1,0:T(8,128)(2,1)} %text_ref.1, f32[64,768]{1,0:T(8,128)} %get-tuple-element.7.total_image_ref, f32[64,768]{1,0:T(8,128)} %get-tuple-element.8.total_text_ref, ...), custom_call_target="tpu_custom_call" | custom-call | tf_op jit(solution)/shard_map/pallas_call | solution.py:443

commit v4 on v3

--- a/solution.py
+++ b/solution.py
@@ -118,14 +118,15 @@
             image_ss.at[half, 0, place], image_rs.at[half, 0, back], axes[half][place],
         )
 
-    def pass_image(half, place):
-        for line in (3, 1, 2):
+    def pass_images(place):
+        for line in (1, 2, 3):
             back = AROUND_BACK[line]
-            image_copies[half, back, place] = send(
-                images.at[pl.ds(image_row(half, 0, place), HALF)],
-                images.at[pl.ds(image_row(half, back, place), HALF)],
-                image_ss.at[half, line, place], image_rs.at[half, back, place], axes[1 - half][line],
-            )
+            for half in (0, 1):
+                image_copies[half, back, place] = send(
+                    images.at[pl.ds(image_row(half, 0, place), HALF)],
+                    images.at[pl.ds(image_row(half, back, place), HALF)],
+                    image_ss.at[half, line, place], image_rs.at[half, back, place], axes[1 - half][line],
+                )
 
     def send_text(block, step, first, count, slot):
         source, target = text_row(0, COLUMN.index(block)), text_row(0, COLUMN.index((block - step) % 8))
@@ -141,26 +142,31 @@
             pair_ss.at[place], pair_rs.at[place], twin,
         )
 
-    send_text(0, 2, 0, ROWS, 0)
-    send_text(0, -2, 0, ROWS, 1)
-    for place in (3, 1, 2):
+    send_text(0, 2, HALF, HALF, 0)
+    send_text(0, -2, 0, HALF, 1)
+    for place in (1, 2, 3):
         for half in (0, 1):
             first_image(half, place)
-    send_text(0, 1, 0, ROWS, 2)
-    send_text(0, -1, 0, ROWS, 3)
+    send_text(0, 2, 0, HALF, 2)
+    send_text(0, -2, HALF, HALF, 3)
     hand_text(0)
-    for half in (0, 1):
-        pass_image(half, 0)
+    pass_images(0)
+    send_text(0, 1, 0, ROWS, 4)
+    send_text(0, -1, 0, ROWS, 5)
     for place in (1, 2, 3):
         for half in (0, 1):
             image_copies[half, 0, place].wait_recv()
-            pass_image(half, place)
+        pass_images(place)
     text_copies[2, 0].wait_recv()
-    send_text(2, -1, 0, ROWS, 4)
-    send_text(2, -2, 0, HALF, 5)
+    send_text(2, -1, 0, HALF, 6)
+    send_text(2, -2, 0, HALF, 7)
+    text_copies[6, HALF].wait_recv()
+    send_text(6, 1, HALF, HALF, 8)
+    send_text(6, 2, HALF, HALF, 9)
+    text_copies[2, HALF].wait_recv()
+    send_text(2, -1, HALF, HALF, 10)
     text_copies[6, 0].wait_recv()
-    send_text(6, 1, 0, ROWS, 6)
-    send_text(6, 2, HALF, HALF, 7)
+    send_text(6, 1, 0, HALF, 11)
     hand_text(2)
     hand_text(6)
 
@@ -305,7 +311,8 @@
     wait_lines(2)
     tiles((1, 0), (1, 1), (2, 0), (2, 1))
     for block in (3, 5):
-        text_copies[block, 0].wait_recv()
+        for first in (0, HALF):
+            text_copies[block, first].wait_recv()
         hand_text(block)
     wait_lines(3)
     tiles((3, 0), (3, 1))
@@ -322,7 +329,6 @@
     found_copies = spread(0, found, [twin])
     image_grads(3)
     send_lines(3, 0)
-    send_lines(3, 1)
     text_grads(3)
     image_grads(1)
     send_lines(1, 0)
@@ -334,8 +340,8 @@
     send_mid(5, -1, 0, ROWS, 1)
     image_grads(2)
     send_lines(2, 0)
-    send_lines(1, 1)
-    send_lines(2, 1)
+    for line in (3, 1, 2):
+        send_lines(line, 1)
     text_sums(2)
     send_mid(4, 2, 0, HALF, 2)
     send_mid(4, -2, HALF, HALF, 3)
@@ -431,7 +437,7 @@
             pltpu.VMEM((4, 7, 8, 128), f32),
             pltpu.VMEM((4, 8, 128), f32),
             dma((4,)),
-            dma((2, 4, 4)), dma((2, 4, 4)), dma((8,)), dma((8,)), dma((8,)), dma((8,)),
+            dma((2, 4, 4)), dma((2, 4, 4)), dma((12,)), dma((12,)), dma((8,)), dma((8,)),
             dma((2, 4, 2)), dma((2, 4, 2)), dma((2, 4)), dma((2, 4)),
             dma((4,)), dma((4,)), dma((4,)), dma((4,)), dma((4,)), dma((4,)),
             dma((4, 7)), dma((4, 7)),

time: 49.9 us -> 49.1 us (0.984)
  Pallas kernels: 47.8 us -> 47 us
    pallas_call x1, Pallas kernels: 45.8 us -> 45 us  [local(): pl.pallas_call(kernel, out_shape=(jax.ShapeDtypeStruct((ROWS, WIDTH), f32...]
where the time goes in v4:
time: 49.1 us; the launch traced here: 48.9 us
  Pallas kernels  47 us (96%)
  between operations  1.93 us (4%)
    pallas_call x1, Pallas kernels, local(): pl.pallas_call(kernel, out_shape=(jax.ShapeDtypeStruct((ROWS, WIDTH), f32...  45 us
    pallas_call x1, Pallas kernels, local(): pl.pallas_call(finish, out_shape=(jax.ShapeDtypeStruct((1,), f32), jax.Sh...  2.06 us

profile of v4, /device:TPU:1, one launch (start us, length us, event | category | flops | bytes accessed | tf_op | source)
XLA Modules:
  0.0 48.9 jit_solution(7792038188654570255)
XLA Ops:
  1.9 45.0 %shard_map.75 = (f32[64,768]{1,0:T(8,128)}, f32[64,768]{1,0:T(8,128)}, f32[8,128]{1,0:T(8,128)}) custom-call(bf16[64,768]{1,0:T(8,128)(2,1)} %image_ref.1, bf16[64,768]{1,0:T(8,128)(2,1)} %text_ref.1, f32[1]{0:T(128)S(6)} %copy.8.temp_hbm, f32[1]{0:T(128)S(6)} %copy.9.bias_hbm), custom_call_target="tpu_custom_call" | custom-call | tf_op jit(solution)/shard_map/pallas_call | solution.py:406
  46.9 2.1 %shard_map.76 = (f32[1]{0:T(128)}, f32[64,768]{1,0:T(8,128)}, f32[64,768]{1,0:T(8,128)}, f32[2]{0:T(128)}) custom-call(bf16[64,768]{1,0:T(8,128)(2,1)} %image_ref.1, bf16[64,768]{1,0:T(8,128)(2,1)} %text_ref.1, f32[64,768]{1,0:T(8,128)} %get-tuple-element.7.total_image_ref, f32[64,768]{1,0:T(8,128)} %get-tuple-element.8.total_text_ref, ...), custom_call_target="tpu_custom_call" | custom-call | tf_op jit(solution)/shard_map/pallas_call | solution.py:449

commit v5 on v4

--- a/solution.py
+++ b/solution.py
@@ -16,6 +16,7 @@
 AROUND = (0, 1, 3, 2)
 AROUND_BACK = tuple(AROUND.index(-d % 4) for d in AROUND)
 COLUMN = (0, 1, 7, 6, 2, 4, 3, 5)
+FOUND = (0, 1, 8, 11, 14)
 COLUMN_BACK = tuple(COLUMN.index(-d % 8) for d in COLUMN)
 
 
@@ -51,7 +52,7 @@
     temp_ref, bias_ref, image_ref, text_ref, images, texts, texts_t, slopes, slopes_t, sums,
     image_part, image_own, image_in, image_mid, image_last,
     text_part, text_own, text_in, pair_part, pair_in, text_mid, found_in, found_out,
-    load, image_ss, image_rs, text_ss, text_rs, pair_ss, pair_rs,
+    load, image_ss, image_rs, lines_rs, text_ss, text_rs, pair_ss, pair_rs,
     line_ss, line_rs, last_ss, last_rs, gt_ss, gt_rs, mid_ss, mid_rs, gp_ss, gp_rs, f_ss, f_rs,
 ):
     blk, narrow = lax.axis_index("blk"), lax.axis_index("narrow")
@@ -97,7 +98,6 @@
 
     pl.semaphore_wait(barrier, len(peers))
 
-    started = []
 
     def send(src, dst, send_sem, recv_sem, peer):
         copy = pltpu.make_async_remote_copy(
@@ -105,8 +105,10 @@
             device_id=peer, device_id_type=MESH,
         )
         copy.start()
-        started.append(copy)
         return copy
+
+    def wait_bytes(ref, sem):
+        pltpu.make_async_copy(ref, ref, sem).wait()
 
     image_copies, text_copies, pair_copies = {}, {}, {}
 
@@ -115,7 +117,7 @@
         image_copies[half, 0, back] = send(
             images.at[pl.ds(image_row(half, 0, 0), HALF)],
             images.at[pl.ds(image_row(half, 0, back), HALF)],
-            image_ss.at[half, 0, place], image_rs.at[half, 0, back], axes[half][place],
+            image_ss.at[0], image_rs.at[half, back], axes[half][place],
         )
 
     def pass_images(place):
@@ -125,21 +127,21 @@
                 image_copies[half, back, place] = send(
                     images.at[pl.ds(image_row(half, 0, place), HALF)],
                     images.at[pl.ds(image_row(half, back, place), HALF)],
-                    image_ss.at[half, line, place], image_rs.at[half, back, place], axes[1 - half][line],
+                    image_ss.at[0], lines_rs.at[back], axes[1 - half][line],
                 )
 
     def send_text(block, step, first, count, slot):
         source, target = text_row(0, COLUMN.index(block)), text_row(0, COLUMN.index((block - step) % 8))
         text_copies[(block - step) % 8, first] = send(
             texts.at[pl.ds(source + first, count)], texts.at[pl.ds(target + first, count)],
-            text_ss.at[slot], text_rs.at[slot], column[step % 8],
+            text_ss.at[0], text_rs.at[slot], column[step % 8],
         )
 
     def hand_text(block):
         place = COLUMN.index(block)
         pair_copies[block] = send(
             texts.at[pl.ds(text_row(0, place), ROWS)], texts.at[pl.ds(text_row(1, place), ROWS)],
-            pair_ss.at[place], pair_rs.at[place], twin,
+            pair_ss.at[0], pair_rs.at[place], twin,
         )
 
     send_text(0, 2, HALF, HALF, 0)
@@ -207,9 +209,7 @@
             sums[n] += sum(share[n] for share in shares)
 
     def wait_lines(line):
-        for half in (0, 1):
-            for place in range(4):
-                image_copies[half, line, place].wait_recv()
+        wait_bytes(images.at[pl.ds(line * GROUP, GROUP)], lines_rs.at[line])
 
     def turn_texts(group):
         for block in COLUMN[2 * group : 2 * group + 2]:
@@ -219,19 +219,19 @@
 
     def spread(stage, values, peers):
         found_out[stage] = values
-        return [
-            send(found_out.at[stage], found_in.at[stage, n], f_ss.at[stage, n], f_rs.at[stage, n], peer)
-            for n, peer in enumerate(peers)
-        ]
-
-    def collect(stage, values, copies):
-        for n, copy in enumerate(copies):
-            copy.wait_recv()
-            values = values + found_in[stage, n]
+        first = FOUND[stage]
+        for n, peer in enumerate(peers):
+            send(found_out.at[stage], found_in.at[first + n], f_ss.at[0], f_rs.at[stage], peer)
+
+    def collect(stage, values):
+        first, end = FOUND[stage], FOUND[stage + 1]
+        wait_bytes(found_in.at[pl.ds(first, end - first)], f_rs.at[stage])
+        for n in range(first, end):
+            values = values + found_in[n]
         return values
 
     row = lax.broadcasted_iota(jnp.int32, (8, 128), 0)
-    line_copies, last_copies, gt_copies, mid_copies, gp_copies = {}, {}, {}, {}, {}
+    mid_copies, gp_copies = {}, {}
 
     def image_grads(line):
         rows = slice(line * GROUP, line * GROUP + GROUP)
@@ -245,18 +245,18 @@
         first, count = (0, HALF) if own else (HALF, LINE - HALF)
         back = AROUND_BACK[line]
         for half in (0, 1):
-            line_copies[half, back, own] = send(
+            send(
                 image_part.at[pl.ds(image_row(half, line, 0) + first, count)],
                 image_in.at[half, back, pl.ds(first, count)],
-                line_ss.at[half, line, own], line_rs.at[half, back, own], axes[1 - half][line],
+                line_ss.at[0], line_rs.at[half, own], axes[1 - half][line],
             )
 
     def line_sum(half, own):
         first, count = (0, HALF) if own else (HALF, LINE - HALF)
         row = half * LINE + first
         part = image_own[row : row + count, :]
+        wait_bytes(image_in.at[half, pl.ds(1, 3), pl.ds(first, count)], line_rs.at[half, own])
         for line in (3, 1, 2):
-            line_copies[half, line, own].wait_recv()
             part = part + wide(image_in[half, line, first : first + count, :])
         return part
 
@@ -267,7 +267,7 @@
         text_own[own, :] = part[0:LINE]
         pair_part[own, :] = part[LINE:GROUP].astype(jnp.bfloat16)
         gp_copies[group] = send(
-            pair_part.at[own], pair_in.at[own], gp_ss.at[group], gp_rs.at[group], twin
+            pair_part.at[own], pair_in.at[own], gp_ss.at[0], gp_rs.at[group], twin
         )
 
     def own_rows(block, first=0, count=ROWS):
@@ -284,12 +284,12 @@
     def send_mid(block, step, first, count, slot):
         mid_copies[slot] = send(
             text_part.at[own_rows(block, first, count)], text_mid.at[slot, pl.ds(first, count)],
-            mid_ss.at[slot], mid_rs.at[slot], column[step % 8],
+            mid_ss.at[0], mid_rs.at[slot], column[step % 8],
         )
 
     def send_share(block, slot):
-        gt_copies[slot] = send(
-            text_part.at[own_rows(block)], text_in.at[slot], gt_ss.at[slot], gt_rs.at[slot], column[block]
+        send(
+            text_part.at[own_rows(block)], text_in.at[slot], gt_ss.at[0], gt_rs.at[0], column[block]
         )
 
     def add_mid(block, near, far, first, slot):
@@ -326,14 +326,14 @@
 
     lane_sums = [jnp.sum(sums[n], keepdims=True) for n in range(3)]
     found = jnp.where(row == 0, lane_sums[0], jnp.where(row == 1, lane_sums[1], lane_sums[2]))
-    found_copies = spread(0, found, [twin])
+    spread(0, found, [twin])
     image_grads(3)
     send_lines(3, 0)
     text_grads(3)
     image_grads(1)
     send_lines(1, 0)
-    found = collect(0, found, found_copies)
-    found_copies = spread(1, found, list(column.values()))
+    found = collect(0, found)
+    spread(1, found, list(column.values()))
     text_grads(2)
     text_sums(3)
     send_mid(3, 1, 0, ROWS, 0)
@@ -352,8 +352,8 @@
     send_share(7, 0)
     text_sums(0)
     send_share(1, 1)
-    found = collect(1, found, found_copies)
-    found_copies = spread(2, found, axes[1][1:])
+    found = collect(1, found)
+    spread(2, found, axes[1][1:])
     add_mid(2, 0, 2, 0, 2)
     add_mid(6, 1, 3, HALF, 3)
 
@@ -361,35 +361,42 @@
         image_mid[half] = line_sum(half, 0).astype(jnp.bfloat16)
         for place in (3, 1, 2):
             back = AROUND_BACK[place]
-            last_copies[half, back] = send(
+            send(
                 image_mid.at[half, pl.ds(place * HALF - HALF, HALF)], image_last.at[half, back],
-                last_ss.at[half, place], last_rs.at[half, back], axes[half][place],
+                last_ss.at[0], last_rs.at[half], axes[half][place],
             )
-    found = collect(2, found, found_copies)
-    found_copies = spread(3, found, axes[0][1:])
+    found = collect(2, found)
+    spread(3, found, axes[0][1:])
     ends = [line_sum(half, 1) for half in (0, 1)]
 
     total = text_own[0:ROWS, :]
+    wait_bytes(text_in, gt_rs.at[0])
     for slot in range(4):
-        gt_copies[slot].wait_recv()
         total = total + wide(text_in[slot])
     total_text_ref[...] = total
 
     for half in (0, 1):
         total = ends[half]
+        wait_bytes(image_last.at[half, pl.ds(1, 3)], last_rs.at[half])
         for place in (1, 2, 3):
-            last_copies[half, place].wait_recv()
             total = total + wide(image_last[half, place])
         rows = slice(half * HALF, half * HALF + HALF)
         total_image_ref[rows, :] = total
 
-    found = collect(3, found, found_copies) * (1.0 / float(TOTAL) ** 2)
+    found = collect(3, found) * (1.0 / float(TOTAL) ** 2)
     lane = lax.broadcasted_iota(jnp.int32, (8, 128), 1)
     scale, slope = found[2:3] * temper[:, 0:128], found[1:2]
     scalars_ref[...] = jnp.where(row == 0, found, jnp.where(lane == 0, scale, slope))
 
-    for copy in started:
-        copy.wait_send()
+    wait_bytes(images.at[0 : 30 * HALF], image_ss.at[0])
+    wait_bytes(texts.at[0 : 7 * ROWS], text_ss.at[0])
+    wait_bytes(texts.at[0 : 8 * ROWS], pair_ss.at[0])
+    wait_bytes(image_part.at[0 : 6 * LINE], line_ss.at[0])
+    wait_bytes(image_mid, last_ss.at[0])
+    wait_bytes(text_part.at[0 : 4 * ROWS], gt_ss.at[0])
+    wait_bytes(text_part.at[0 : 3 * ROWS], mid_ss.at[0])
+    wait_bytes(pair_part, gp_ss.at[0])
+    wait_bytes(found_in.at[0 : FOUND[4]], f_ss.at[0])
 
 
 def finish(image_ref, text_ref, total_image_ref, total_text_ref, scalars_ref, mean_ref, grad_image_ref, grad_text_ref, pair_ref):
@@ -434,13 +441,12 @@
             pltpu.VMEM((8 * ROWS, WIDTH), bf16),
             pltpu.VMEM((8 * ROWS, WIDTH), bf16),
             pltpu.VMEM((4, ROWS, WIDTH), bf16),
-            pltpu.VMEM((4, 7, 8, 128), f32),
+            pltpu.VMEM((14, 8, 128), f32),
             pltpu.VMEM((4, 8, 128), f32),
             dma((4,)),
-            dma((2, 4, 4)), dma((2, 4, 4)), dma((12,)), dma((12,)), dma((8,)), dma((8,)),
-            dma((2, 4, 2)), dma((2, 4, 2)), dma((2, 4)), dma((2, 4)),
-            dma((4,)), dma((4,)), dma((4,)), dma((4,)), dma((4,)), dma((4,)),
-            dma((4, 7)), dma((4, 7)),
+            dma((1,)), dma((2, 4)), dma((4,)), dma((1,)), dma((12,)), dma((1,)), dma((8,)),
+            dma((1,)), dma((2, 2)), dma((1,)), dma((2,)), dma((1,)), dma((1,)),
+            dma((1,)), dma((4,)), dma((1,)), dma((4,)), dma((1,)), dma((4,)),
         ],
         compiler_params=pltpu.CompilerParams(
             collective_id=0, has_side_effects=True, vmem_limit_bytes=56 * 1024 * 1024

time: 49.1 us -> 47.5 us (0.967)
  Pallas kernels: 47 us -> 45.4 us
    pallas_call x1, Pallas kernels: 45 us -> 43.3 us  [local(): pl.pallas_call(kernel, out_shape=(jax.ShapeDtypeStruct((ROWS, WIDTH), f32...]
where the time goes in v5:
time: 47.5 us; the launch traced here: 47.3 us
  Pallas kernels  45.4 us (96%)
  between operations  1.93 us (4%)
    pallas_call x1, Pallas kernels, local(): pl.pallas_call(kernel, out_shape=(jax.ShapeDtypeStruct((ROWS, WIDTH), f32...  43.3 us
    pallas_call x1, Pallas kernels, local(): pl.pallas_call(finish, out_shape=(jax.ShapeDtypeStruct((1,), f32), jax.Sh...  2.06 us

profile of v5, /device:TPU:1, one launch (start us, length us, event | category | flops | bytes accessed | tf_op | source)
XLA Modules:
  0.0 47.3 jit_solution(8515734014165855803)
XLA Ops:
  1.9 43.3 %shard_map.75 = (f32[64,768]{1,0:T(8,128)}, f32[64,768]{1,0:T(8,128)}, f32[8,128]{1,0:T(8,128)}) custom-call(bf16[64,768]{1,0:T(8,128)(2,1)} %image_ref.1, bf16[64,768]{1,0:T(8,128)(2,1)} %text_ref.1, f32[1]{0:T(128)S(6)} %copy.8.temp_hbm, f32[1]{0:T(128)S(6)} %copy.9.bias_hbm), custom_call_target="tpu_custom_call" | custom-call | tf_op jit(solution)/shard_map/pallas_call | solution.py:413
  45.2 2.1 %shard_map.76 = (f32[1]{0:T(128)}, f32[64,768]{1,0:T(8,128)}, f32[64,768]{1,0:T(8,128)}, f32[2]{0:T(128)}) custom-call(bf16[64,768]{1,0:T(8,128)(2,1)} %image_ref.1, bf16[64,768]{1,0:T(8,128)(2,1)} %text_ref.1, f32[64,768]{1,0:T(8,128)} %get-tuple-element.7.total_image_ref, f32[64,768]{1,0:T(8,128)} %get-tuple-element.8.total_text_ref, ...), custom_call_target="tpu_custom_call" | custom-call | tf_op jit(solution)/shard_map/pallas_call | solution.py:455

commit v6 on v5

--- a/solution.py
+++ b/solution.py
@@ -69,10 +69,6 @@
     column = {d: device(0, 0, d, 0) for d in range(1, 8)}
     twin = device(0, 0, 0, 1)
 
-    barrier = pltpu.get_barrier_semaphore()
-    peers = [axes[0][3], axes[1][3], *axes[0][1:3], *axes[1][1:3], *column.values(), twin]
-    for peer in peers:
-        pl.semaphore_signal(barrier, inc=1, device_id=peer, device_id_type=MESH)
     loads = [
         pltpu.make_async_copy(image_hbm, image_ref, load.at[0]),
         pltpu.make_async_copy(text_hbm, text_ref, load.at[1]),
@@ -81,23 +77,19 @@
     ]
     for copy in loads:
         copy.start()
-    sums[...] = jnp.zeros_like(sums)
-    for copy in loads:
-        copy.wait()
-    temper = jnp.exp(jnp.full((1, 256), temp_ref[0], jnp.float32))
-    offset = jnp.full((1, 256), bias_ref[0], jnp.float32)
-    temper2, offset2 = temper * LOG2E, offset * LOG2E
-    temper3 = jnp.concatenate([temper] * 3, axis=1)
+    barrier = pltpu.get_barrier_semaphore()
+    peers = [axes[0][3], axes[1][3], *axes[0][1:3], *axes[1][1:3], *column.values(), twin]
+    for peer in peers:
+        pl.semaphore_signal(barrier, inc=1, device_id=peer, device_id_type=MESH)
+
+    loads[0].wait()
     image = wide(image_ref[...])
     image = (image * row_scale(image)).astype(jnp.bfloat16)
     for half in (0, 1):
         row = image_row(half, 0, 0)
         images[row : row + HALF, :] = image[half * HALF : half * HALF + HALF]
-    text = wide(text_ref[...])
-    texts[0:ROWS, :] = (text * row_scale(text)).astype(jnp.bfloat16)
 
     pl.semaphore_wait(barrier, len(peers))
-
 
     def send(src, dst, send_sem, recv_sem, peer):
         copy = pltpu.make_async_remote_copy(
@@ -110,21 +102,21 @@
     def wait_bytes(ref, sem):
         pltpu.make_async_copy(ref, ref, sem).wait()
 
-    image_copies, text_copies, pair_copies = {}, {}, {}
+    text_copies = {}
 
     def first_image(half, place):
         back = AROUND_BACK[place]
-        image_copies[half, 0, back] = send(
+        send(
             images.at[pl.ds(image_row(half, 0, 0), HALF)],
             images.at[pl.ds(image_row(half, 0, back), HALF)],
-            image_ss.at[0], image_rs.at[half, back], axes[half][place],
+            image_ss.at[0], image_rs.at[back], axes[half][place],
         )
 
     def pass_images(place):
         for line in (1, 2, 3):
             back = AROUND_BACK[line]
             for half in (0, 1):
-                image_copies[half, back, place] = send(
+                send(
                     images.at[pl.ds(image_row(half, 0, place), HALF)],
                     images.at[pl.ds(image_row(half, back, place), HALF)],
                     image_ss.at[0], lines_rs.at[back], axes[1 - half][line],
@@ -139,25 +131,36 @@
 
     def hand_text(block):
         place = COLUMN.index(block)
-        pair_copies[block] = send(
+        send(
             texts.at[pl.ds(text_row(0, place), ROWS)], texts.at[pl.ds(text_row(1, place), ROWS)],
-            pair_ss.at[0], pair_rs.at[place], twin,
-        )
-
-    send_text(0, 2, HALF, HALF, 0)
-    send_text(0, -2, 0, HALF, 1)
+            pair_ss.at[0], pair_rs.at[place // 2], twin,
+        )
+
     for place in (1, 2, 3):
         for half in (0, 1):
             first_image(half, place)
+    loads[1].wait()
+    text = wide(text_ref[...])
+    texts[0:ROWS, :] = (text * row_scale(text)).astype(jnp.bfloat16)
+    send_text(0, 2, HALF, HALF, 0)
+    send_text(0, -2, 0, HALF, 1)
     send_text(0, 2, 0, HALF, 2)
     send_text(0, -2, HALF, HALF, 3)
     hand_text(0)
     pass_images(0)
     send_text(0, 1, 0, ROWS, 4)
     send_text(0, -1, 0, ROWS, 5)
+
+    for copy in loads[2:]:
+        copy.wait()
+    temper = jnp.exp(jnp.full((1, 256), temp_ref[0], jnp.float32))
+    offset = jnp.full((1, 256), bias_ref[0], jnp.float32)
+    temper2, offset2 = temper * LOG2E, offset * LOG2E
+    temper3 = jnp.concatenate([temper] * 3, axis=1)
+    sums[...] = jnp.zeros_like(sums)
+
     for place in (1, 2, 3):
-        for half in (0, 1):
-            image_copies[half, 0, place].wait_recv()
+        wait_bytes(images.at[pl.ds(0, 2 * HALF)], image_rs.at[place])
         pass_images(place)
     text_copies[2, 0].wait_recv()
     send_text(2, -1, 0, HALF, 6)
@@ -212,8 +215,7 @@
         wait_bytes(images.at[pl.ds(line * GROUP, GROUP)], lines_rs.at[line])
 
     def turn_texts(group):
-        for block in COLUMN[2 * group : 2 * group + 2]:
-            pair_copies[block].wait_recv()
+        wait_bytes(texts.at[pl.ds(group * GROUP + LINE, LINE)], pair_rs.at[group])
         rows = slice(group * GROUP, group * GROUP + GROUP)
         texts_t[:, rows] = texts[rows, :].T
 
@@ -241,23 +243,22 @@
         else:
             image_part[rows, :] = part.astype(jnp.bfloat16)
 
-    def send_lines(line, own):
-        first, count = (0, HALF) if own else (HALF, LINE - HALF)
-        back = AROUND_BACK[line]
+    def send_line(line, place):
+        first, back = place * HALF, AROUND_BACK[line]
         for half in (0, 1):
             send(
-                image_part.at[pl.ds(image_row(half, line, 0) + first, count)],
-                image_in.at[half, back, pl.ds(first, count)],
-                line_ss.at[0], line_rs.at[half, own], axes[1 - half][line],
+                image_part.at[pl.ds(image_row(half, line, place), HALF)],
+                image_in.at[half, back, pl.ds(first, HALF)],
+                line_ss.at[0], line_rs.at[half, place], axes[1 - half][line],
             )
 
-    def line_sum(half, own):
-        first, count = (0, HALF) if own else (HALF, LINE - HALF)
+    def line_sum(half, place):
+        first = place * HALF
         row = half * LINE + first
-        part = image_own[row : row + count, :]
-        wait_bytes(image_in.at[half, pl.ds(1, 3), pl.ds(first, count)], line_rs.at[half, own])
+        part = image_own[row : row + HALF, :]
+        wait_bytes(image_in.at[half, pl.ds(1, 3), pl.ds(first, HALF)], line_rs.at[half, place])
         for line in (3, 1, 2):
-            part = part + wide(image_in[half, line, first : first + count, :])
+            part = part + wide(image_in[half, line, first : first + HALF, :])
         return part
 
     def text_grads(group):
@@ -328,10 +329,12 @@
     found = jnp.where(row == 0, lane_sums[0], jnp.where(row == 1, lane_sums[1], lane_sums[2]))
     spread(0, found, [twin])
     image_grads(3)
-    send_lines(3, 0)
+    for place in (3, 1, 2):
+        send_line(3, place)
     text_grads(3)
     image_grads(1)
-    send_lines(1, 0)
+    for place in (3, 1, 2):
+        send_line(1, place)
     found = collect(0, found)
     spread(1, found, list(column.values()))
     text_grads(2)
@@ -339,9 +342,10 @@
     send_mid(3, 1, 0, ROWS, 0)
     send_mid(5, -1, 0, ROWS, 1)
     image_grads(2)
-    send_lines(2, 0)
+    for place in (3, 1, 2):
+        send_line(2, place)
     for line in (3, 1, 2):
-        send_lines(line, 1)
+        send_line(line, 0)
     text_sums(2)
     send_mid(4, 2, 0, HALF, 2)
     send_mid(4, -2, HALF, HALF, 3)
@@ -357,17 +361,17 @@
     add_mid(2, 0, 2, 0, 2)
     add_mid(6, 1, 3, HALF, 3)
 
-    for half in (0, 1):
-        image_mid[half] = line_sum(half, 0).astype(jnp.bfloat16)
-        for place in (3, 1, 2):
-            back = AROUND_BACK[place]
+    for place in (3, 1, 2):
+        for half in (0, 1):
+            first, back = place * HALF - HALF, AROUND_BACK[place]
+            image_mid[half, first : first + HALF, :] = line_sum(half, place).astype(jnp.bfloat16)
             send(
-                image_mid.at[half, pl.ds(place * HALF - HALF, HALF)], image_last.at[half, back],
+                image_mid.at[half, pl.ds(first, HALF)], image_last.at[half, back],
                 last_ss.at[0], last_rs.at[half], axes[half][place],
             )
     found = collect(2, found)
     spread(3, found, axes[0][1:])
-    ends = [line_sum(half, 1) for half in (0, 1)]
+    ends = [line_sum(half, 0) for half in (0, 1)]
 
     total = text_own[0:ROWS, :]
     wait_bytes(text_in, gt_rs.at[0])
@@ -444,8 +448,8 @@
             pltpu.VMEM((14, 8, 128), f32),
             pltpu.VMEM((4, 8, 128), f32),
             dma((4,)),
-            dma((1,)), dma((2, 4)), dma((4,)), dma((1,)), dma((12,)), dma((1,)), dma((8,)),
-            dma((1,)), dma((2, 2)), dma((1,)), dma((2,)), dma((1,)), dma((1,)),
+            dma((1,)), dma((4,)), dma((4,)), dma((1,)), dma((12,)), dma((1,)), dma((4,)),
+            dma((1,)), dma((2, 4)), dma((1,)), dma((2,)), dma((1,)), dma((1,)),
             dma((1,)), dma((4,)), dma((1,)), dma((4,)), dma((1,)), dma((4,)),
         ],
         compiler_params=pltpu.CompilerParams(

time: 47.5 us -> 47.4 us (level)
  no operation moved by 1% of the time
where the time goes in v6:
time: 47.4 us; the launch traced here: 47.2 us
  Pallas kernels  45.3 us (96%)
  between operations  1.93 us (4%)
    pallas_call x1, Pallas kernels, local(): pl.pallas_call(kernel, out_shape=(jax.ShapeDtypeStruct((ROWS, WIDTH), f32...  43.2 us
    pallas_call x1, Pallas kernels, local(): pl.pallas_call(finish, out_shape=(jax.ShapeDtypeStruct((1,), f32), jax.Sh...  2.06 us

profile of v6, /device:TPU:1, one launch (start us, length us, event | category | flops | bytes accessed | tf_op | source)
XLA Modules:
  0.0 47.2 jit_solution(14868743178461483965)
XLA Ops:
  1.9 43.2 %shard_map.75 = (f32[64,768]{1,0:T(8,128)}, f32[64,768]{1,0:T(8,128)}, f32[8,128]{1,0:T(8,128)}) custom-call(bf16[64,768]{1,0:T(8,128)(2,1)} %image_ref.1, bf16[64,768]{1,0:T(8,128)(2,1)} %text_ref.1, f32[1]{0:T(128)S(6)} %copy.8.temp_hbm, f32[1]{0:T(128)S(6)} %copy.9.bias_hbm), custom_call_target="tpu_custom_call" | custom-call | tf_op jit(solution)/shard_map/pallas_call | solution.py:417
  45.2 2.1 %shard_map.76 = (f32[1]{0:T(128)}, f32[64,768]{1,0:T(8,128)}, f32[64,768]{1,0:T(8,128)}, f32[2]{0:T(128)}) custom-call(bf16[64,768]{1,0:T(8,128)(2,1)} %image_ref.1, bf16[64,768]{1,0:T(8,128)(2,1)} %text_ref.1, f32[64,768]{1,0:T(8,128)} %get-tuple-element.7.total_image_ref, f32[64,768]{1,0:T(8,128)} %get-tuple-element.8.total_text_ref, ...), custom_call_target="tpu_custom_call" | custom-call | tf_op jit(solution)/shard_map/pallas_call | solution.py:459

commit v7 on v6

--- a/solution.py
+++ b/solution.py
@@ -48,7 +48,7 @@
 
 def kernel(
     image_hbm, text_hbm, temp_hbm, bias_hbm,
-    total_image_ref, total_text_ref, scalars_ref,
+    grad_image_out, grad_text_out, scalars_ref,
     temp_ref, bias_ref, image_ref, text_ref, images, texts, texts_t, slopes, slopes_t, sums,
     image_part, image_own, image_in, image_mid, image_last,
     text_part, text_own, text_in, pair_part, pair_in, text_mid, found_in, found_out,
@@ -377,7 +377,7 @@
     wait_bytes(text_in, gt_rs.at[0])
     for slot in range(4):
         total = total + wide(text_in[slot])
-    total_text_ref[...] = total
+    grad_text_out[...] = back_rows(wide(text_ref[...]), total)
 
     for half in (0, 1):
         total = ends[half]
@@ -385,7 +385,7 @@
         for place in (1, 2, 3):
             total = total + wide(image_last[half, place])
         rows = slice(half * HALF, half * HALF + HALF)
-        total_image_ref[rows, :] = total
+        grad_image_out[rows, :] = back_rows(wide(image_ref[rows, :]), total)
 
     found = collect(3, found) * (1.0 / float(TOTAL) ** 2)
     lane = lax.broadcasted_iota(jnp.int32, (8, 128), 1)
@@ -403,9 +403,9 @@
     wait_bytes(found_in.at[0 : FOUND[4]], f_ss.at[0])
 
 
-def finish(image_ref, text_ref, total_image_ref, total_text_ref, scalars_ref, mean_ref, grad_image_ref, grad_text_ref, pair_ref):
-    grad_image_ref[...] = back_rows(wide(image_ref[...]), total_image_ref[...])
-    grad_text_ref[...] = back_rows(wide(text_ref[...]), total_text_ref[...])
+def finish(image_in, text_in, scalars_ref, mean_ref, image_out, text_out, pair_ref):
+    image_out[...] = image_in[...]
+    text_out[...] = text_in[...]
     mean_ref[...] = scalars_ref[0, 0:1]
     pair_ref[...] = scalars_ref[1, 0:2]
 
@@ -414,7 +414,7 @@
     bf16, f32 = jnp.bfloat16, jnp.float32
     vmem, hbm = pl.BlockSpec(memory_space=pltpu.VMEM), pl.BlockSpec(memory_space=pltpu.HBM)
     dma = pltpu.SemaphoreType.DMA
-    total_image, total_text, scalars = pl.pallas_call(
+    grad_image, grad_text, scalars = pl.pallas_call(
         kernel,
         out_shape=(
             jax.ShapeDtypeStruct((ROWS, WIDTH), f32),
@@ -464,9 +464,9 @@
             jax.ShapeDtypeStruct((ROWS, WIDTH), f32),
             jax.ShapeDtypeStruct((2,), f32),
         ),
-        in_specs=[vmem] * 5,
+        in_specs=[vmem] * 3,
         out_specs=(vmem,) * 4,
-    )(image_emb, text_emb, total_image, total_text, scalars)
+    )(grad_image, grad_text, scalars)
     return (mean_loss, grad_image, grad_text, scalar_grads)
 
 

time: 47.4 us -> 47.4 us (level)
  no operation moved by 1% of the time
where the time goes in v7:
time: 47.4 us; the launch traced here: 47.3 us
  Pallas kernels  45.4 us (96%)
  between operations  1.93 us (4%)
    pallas_call x1, Pallas kernels, local(): pl.pallas_call(kernel, out_shape=(jax.ShapeDtypeStruct((ROWS, WIDTH), f32...  43.6 us
    pallas_call x1, Pallas kernels, local(): pl.pallas_call(finish, out_shape=(jax.ShapeDtypeStruct((1,), f32), jax.Sh...  1.78 us

profile of v7, /device:TPU:1, one launch (start us, length us, event | category | flops | bytes accessed | tf_op | source)
XLA Modules:
  0.0 47.3 jit_solution(16053555932239049683)
XLA Ops:
  1.9 43.6 %shard_map.75 = (f32[64,768]{1,0:T(8,128)}, f32[64,768]{1,0:T(8,128)}, f32[8,128]{1,0:T(8,128)}) custom-call(bf16[64,768]{1,0:T(8,128)(2,1)} %image_hbm.1, bf16[64,768]{1,0:T(8,128)(2,1)} %text_hbm.1, f32[1]{0:T(128)S(6)} %copy.8.temp_hbm, f32[1]{0:T(128)S(6)} %copy.9.bias_hbm), custom_call_target="tpu_custom_call" | custom-call | tf_op jit(solution)/shard_map/pallas_call | solution.py:417
  45.5 1.8 %shard_map.76 = (f32[1]{0:T(128)}, f32[64,768]{1,0:T(8,128)}, f32[64,768]{1,0:T(8,128)}, f32[2]{0:T(128)}) custom-call(f32[64,768]{1,0:T(8,128)} %get-tuple-element.7.image_in, f32[64,768]{1,0:T(8,128)} %get-tuple-element.8.text_in, f32[8,128]{1,0:T(8,128)} %get-tuple-element.9.scalars_ref), custom_call_target="tpu_custom_call" | custom-call | tf_op jit(solution)/shard_map/pallas_call | solution.py:459
